TPU v7x, 128 devices: a whole 4x4x4 slice. The times are simulated.
128 devices in a mesh: gx: 8 (over y, core), gy: 16 (over x, z).
Axes of the slice: x: 4, y: 4, z: 4, core: 2. Of those that a mesh axis runs over, the one named last changes fastest.
Arguments:
- soil_now: float32 [48, 256, 4096], P(None, 'gx', 'gy'), may hold values from -6 to 6
- soil_old: float32 [48, 256, 4096], P(None, 'gx', 'gy'), may hold values from -6 to 6
- kappa: float32 [48, 256, 4096], P(None, 'gx', 'gy'), may hold values from 0.15 to 0.3
- force_prev: float32 [256, 4096], P('gx', 'gy'), may hold values from -6 to 6
- storey_disp: float32 [32, 262144], P(None, ('gx', 'gy')), may hold values from -6 to 6
- storey_vel: float32 [32, 262144], P(None, ('gx', 'gy')), may hold values from -3 to 3
- stiffness: float32 [32, 262144], P(None, ('gx', 'gy')), may hold values from 0.03 to 0.5
- branch_flag: int32 [32, 262144], P(None, ('gx', 'gy')), may hold values from 0 to 2
- footprint_tile: int32 [262144, 1], P(('gx', 'gy')), may hold values from 0 to 127; in each aligned block of 2048 rows (0 to 2047, 2048 to 4095, ...) at most 32 rows name the same one
- footprint_cell: int32 [262144], P(('gx', 'gy')), may hold values from 0 to 8191
Outputs:
- soil_next: float32 [48, 256, 4096], P(None, 'gx', 'gy')
- soil_before: float32 [48, 256, 4096], P(None, 'gx', 'gy')
- disp_next: float32 [32, 262144], P(None, ('gx', 'gy'))
- vel_next: float32 [32, 262144], P(None, ('gx', 'gy'))
- base_shear: float32 [256, 4096], P('gx', 'gy')
Inputs may be any that keep to these rules, and one draw needn't show every extreme that they name: `footprint_tile`: among the 2048 buildings of one device at most 32 stand on one tile, and in every draw some tile receives exactly 32 of them from some device.
All inputs are finite; a program needn't handle non-finite values.
Results may differ from a plain program's by a relative error of at most 0.00023.
Values sent between devices are 32-bit elements; how exact they have to be, the bound alone decides.
A program may use at most 128 MiB of HBM per device.

v0:
```python
import functools

import jax
import jax.numpy as jnp
from jax import lax
from jax.experimental import pallas as pl
from jax.experimental.pallas import tpu as pltpu
from jax.sharding import PartitionSpec as P

STEPS = 8
force_gain = 0.05
f32, bf16 = jnp.float32, jnp.bfloat16
CHUNKS = 2
SLOTS = 32
COEF, BASE, ROW, COL, WIDE = 0, 256, 288, 320, 384
BLOCK = 256
MESH = pl.DeviceIdType.MESH


def split(x):
    high = x.astype(bf16)
    return high, (x - high.astype(f32)).astype(bf16)


def nt(a, b):
    return lax.dot_general(a, b, (((1,), (1,)), ((), ())), preferred_element_type=f32)


def nn(a, b):
    return jnp.dot(a, b, preferred_element_type=f32)


def kernel(
    n_gx,
    n_gy,
    depth,
    rows,
    tile_ref,
    cell_ref,
    now_hbm,
    old_hbm,
    kappa_hbm,
    force_hbm,
    disp_hbm,
    vel_hbm,
    stiff_hbm,
    flag_hbm,
    next_hbm,
    before_hbm,
    disp_out,
    vel_out,
    base_out,
    soil_a,
    soil_b,
    kappa,
    force,
    disp,
    vel,
    stiff,
    flag,
    disp_new,
    vel_new,
    base,
    x_send,
    x_recv,
    y_send,
    y_recv,
    marks,
    rank_ref,
    payload,
    recv_one,
    mid_one,
    request,
    request_t,
    hot,
    motion,
    picked,
    reply,
    recv_two,
    mid_two,
    answer,
    in_sem,
    out_sem,
    halo_send,
    halo_recv,
    one_send,
    one_recv,
    two_send,
    two_recv,
    three_send,
    three_recv,
    four_send,
    four_recv,
):
    gx, gy = lax.axis_index("gx"), lax.axis_index("gy")
    tiles = n_gx * n_gy
    count = tile_ref.shape[1]
    planes = depth // CHUNKS
    cells = depth * rows

    loads = []
    pairs = (
        (now_hbm, soil_a.at[pl.ds(0, cells)]),
        (old_hbm, soil_b.at[pl.ds(0, cells)]),
        (kappa_hbm, kappa),
        (force_hbm, force),
        (disp_hbm, disp),
        (vel_hbm, vel),
        (stiff_hbm, stiff),
        (flag_hbm, flag),
    )
    for i, (source, target) in enumerate(pairs):
        copy = pltpu.make_async_copy(source, target, in_sem.at[i])
        copy.start()
        loads.append(copy)

    barrier = pltpu.get_barrier_semaphore()
    for k in range(1, n_gx):
        pl.semaphore_signal(
            barrier, inc=1, device_id=(lax.rem(gx + k, n_gx), gy), device_id_type=MESH
        )
    for k in range(1, n_gy):
        pl.semaphore_signal(
            barrier, inc=1, device_id=(gx, lax.rem(gy + k, n_gy)), device_id_type=MESH
        )

    soil_a[pl.ds(cells, rows), :] = jnp.zeros((rows, 256), f32)
    soil_b[pl.ds(cells, rows), :] = jnp.zeros((rows, 256), f32)
    has = (gx > 0, gx < n_gx - 1, gy > 0, gy < n_gy - 1)
    for side in range(4):

        @pl.when(jnp.logical_not(has[side]))
        def _():
            if side < 2:
                x_recv[:, side] = jnp.zeros((STEPS, 2, depth, 128), f32)
            else:
                y_recv[:, :, side - 2] = jnp.zeros((STEPS, CHUNKS, rows, 128), f32)

    neighbour = ((gx - 1, gy), (gx + 1, gy), (gx, gy - 1), (gx, gy + 1))

    def halo(slot, chunk, side):
        other = side ^ 1
        if side < 2:
            source = x_send.at[slot, side, :, pl.ds(chunk * planes, planes)]
            target = x_recv.at[slot, other, :, pl.ds(chunk * planes, planes)]
        else:
            source = y_send.at[slot, chunk, side - 2]
            target = y_recv.at[slot, chunk, other - 2]
        return pltpu.make_async_remote_copy(
            src_ref=source,
            dst_ref=target,
            send_sem=halo_send.at[slot, chunk, side],
            recv_sem=halo_recv.at[slot, chunk, other],
            device_id=neighbour[side],
            device_id_type=MESH,
        )

    def arrival(slot, chunk, side):
        if side < 2:
            target = x_recv.at[slot, side, :, pl.ds(chunk * planes, planes)]
        else:
            target = y_recv.at[slot, chunk, side - 2]
        return pltpu.make_async_remote_copy(
            src_ref=target,
            dst_ref=target,
            send_sem=halo_send.at[slot, chunk, side],
            recv_sem=halo_recv.at[slot, chunk, side],
            device_id=neighbour[side],
            device_id_type=MESH,
        )

    def send_halo(slot, chunk):
        for side in range(4):

            @pl.when(has[side])
            def _():
                halo(slot, chunk, side).start()

    def wait_halo(slot, chunk):
        for side in range(4):

            @pl.when(has[side])
            def _():
                arrival(slot, chunk, side).wait_recv()

    def edge_rows(slot, z, i, value):
        x_send[slot, 0, i, pl.ds(z, 1), :] = value[0:1]
        x_send[slot, 1, i, pl.ds(z, 1), :] = value[rows - 1 : rows]

    lane = lax.broadcasted_iota(jnp.int32, (rows, 128), 1)
    line = lax.broadcasted_iota(jnp.int32, (rows, 128), 0)

    def pack(edges, z, low, high):
        return (
            jnp.where(lane == z, jnp.broadcast_to(low[:, 0:1], (rows, 128)), edges[0]),
            jnp.where(lane == z, jnp.broadcast_to(high[:, 127:128], (rows, 128)), edges[1]),
        )

    def plane(z):
        return pl.ds(pl.multiple_of(z * rows, rows), rows)

    def advance_plane(slot, chunk, here, there, z, edges, top):
        above_z = 0 if top else z - 1
        fresh = []
        halves = [here[plane(z), 0:128], here[plane(z), 128:256]]
        turned = [pltpu.roll(half, 1, 1) for half in halves]
        back = [pltpu.roll(half, 127, 1) for half in halves]
        west = pltpu.roll(y_recv[slot, chunk, 0], 128 - z, 1)
        east = pltpu.roll(y_recv[slot, chunk, 1], 127 - z, 1)
        lows = [jnp.where(lane == 0, west, turned[0]), jnp.where(lane == 0, turned[0], turned[1])]
        highs = [jnp.where(lane == 127, back[1], back[0]), jnp.where(lane == 127, east, back[1])]
        for i in range(2):
            cols = pl.ds(i * 128, 128)
            centre = halves[i]
            north = jnp.where(
                line == 0, x_recv[slot, 0, i, pl.ds(z, 1), :], pltpu.roll(centre, 1, 0)
            )
            south = jnp.where(
                line == rows - 1,
                x_recv[slot, 1, i, pl.ds(z, 1), :],
                pltpu.roll(centre, rows - 1, 0),
            )
            above = here[plane(above_z), cols]
            below = here[plane(z + 1), cols]
            spread = (north + south) + (lows[i] + highs[i]) + (above + below) - 6.0 * centre
            value = 2.0 * centre - there[plane(z), cols] + kappa[plane(z), cols] * spread
            if top:
                value = value + force_gain * force[:, cols]
            there[plane(z), cols] = value
            if slot < STEPS - 1:
                edge_rows(slot + 1, z, i, value)
            fresh.append(value)
            if top:
                motion[i, pl.ds(slot, rows, stride=STEPS), :] = value
        return pack(edges, z, fresh[0], fresh[1])

    def advance(step, chunk, here, there):
        wait_halo(step, chunk)
        first = chunk * planes
        edges = (jnp.zeros((rows, 128), f32), jnp.zeros((rows, 128), f32))
        if chunk == 0:
            edges = advance_plane(step, chunk, here, there, 0, edges, True)
        edges = lax.fori_loop(
            max(first, 1),
            first + planes,
            lambda z, kept: advance_plane(step, chunk, here, there, z, kept, False),
            edges,
        )
        if step < STEPS - 1:
            y_send[step + 1, chunk, 0] = edges[0]
            y_send[step + 1, chunk, 1] = edges[1]
            send_halo(step + 1, chunk)

    loads[0].wait()
    for chunk in range(CHUNKS):
        first = chunk * planes

        def first_edges(z, kept):
            low, high = soil_a[plane(z), 0:128], soil_a[plane(z), 128:256]
            edge_rows(0, z, 0, low)
            edge_rows(0, z, 1, high)
            return pack(kept, z, low, high)

        edges = lax.fori_loop(
            first,
            first + planes,
            first_edges,
            (jnp.zeros((rows, 128), f32), jnp.zeros((rows, 128), f32)),
        )
        y_send[0, chunk, 0] = edges[0]
        y_send[0, chunk, 1] = edges[1]
    pl.semaphore_wait(barrier, n_gx + n_gy - 2)
    for chunk in range(CHUNKS):
        send_halo(0, chunk)

    for copy in loads[4:]:
        copy.wait()
    stiff[...] = stiff[...] * jnp.where(
        flag[...] == 0, 1.0, jnp.where(flag[...] == 1, 0.6, 0.15)
    ).astype(f32)
    payload[...] = jnp.zeros((tiles, WIDE), f32)
    before = (
        lax.broadcasted_iota(jnp.int32, (BLOCK, BLOCK), 0)
        < lax.broadcasted_iota(jnp.int32, (BLOCK, BLOCK), 1)
    ).astype(f32).astype(bf16)
    tile_number = lax.broadcasted_iota(jnp.int32, (tiles, BLOCK), 0)
    slot_number = lax.broadcasted_iota(jnp.int32, (SLOTS, BLOCK), 0)
    storey = lax.broadcasted_iota(jnp.int32, (8, BLOCK), 0)

    def list_block(j, used):
        cols = pl.ds(pl.multiple_of(j * BLOCK, BLOCK), BLOCK)
        chosen = (tile_number == tile_ref[:, cols]).astype(f32)
        mark = chosen.astype(bf16)
        marks[:, cols] = mark
        earlier = nn(mark, before) + used
        rank = jnp.sum(chosen * earlier, 0, keepdims=True).astype(jnp.int32)
        rank_ref[:, cols] = rank
        k = stiff[0:8, cols]
        of_disp = jnp.zeros((8, BLOCK), f32)
        of_vel = jnp.zeros((8, BLOCK), f32)
        coefs = jnp.zeros((8, BLOCK), f32)
        for step in reversed(range(STEPS)):
            of_vel = of_vel + of_disp
            pull = k * (jnp.where(storey == 0, 1.0, pltpu.roll(of_vel, 1, 0)) - of_vel)
            of_disp = of_disp + pull - jnp.where(storey == 7, 0.0, pltpu.roll(pull, 7, 0))
            coefs = jnp.where(storey == step, -pull[0:1], coefs)
        scale = 1.0 / STEPS
        constant = scale * jnp.sum(
            of_disp * disp[0:8, cols] + of_vel * vel[0:8, cols], 0, keepdims=True
        )
        coefs = scale * coefs
        row = (cell_ref[:, cols] // 256).astype(f32)
        col = (cell_ref[:, cols] % 256).astype(f32)
        here = slot_number == rank

        def spread_out(coef, single):
            parts = [jnp.where(rank == d, coef, 0.0) for d in range(SLOTS)]
            parts += [jnp.where(here, value, 0.0) for value in single]
            parts.append(jnp.zeros((SLOTS * (4 - len(single)), BLOCK), f32))
            return jnp.concatenate(parts, 0).astype(bf16)

        coef_high = coefs.astype(bf16).astype(f32)
        constant_high = constant.astype(bf16).astype(f32)
        payload[...] += nt(mark, spread_out(coef_high, (constant_high, row, col))) + nt(
            mark, spread_out(coefs - coef_high, (constant - constant_high,))
        )
        return used + jnp.sum(chosen, 1, keepdims=True)

    lax.fori_loop(0, count // BLOCK, list_block, jnp.zeros((tiles, 1), f32))

    def along_x(k):
        return lax.rem(gx + k, n_gx)

    def along_y(k):
        return lax.rem(gy + k, n_gy)

    def stage_x(source_of, target, send_sem, recv_sem):
        copies = []
        for k in range(1, n_gx):
            peer = along_x(k)
            copy = pltpu.make_async_remote_copy(
                src_ref=source_of(peer),
                dst_ref=target.at[gx],
                send_sem=send_sem.at[k],
                recv_sem=recv_sem.at[k],
                device_id=(peer, gy),
                device_id_type=MESH,
            )
            copy.start()
            copies.append(copy)
        return copies

    def stage_y(source_of, target, send_sem, recv_sem):
        copies = []
        for k in range(1, n_gy):
            peer = along_y(k)
            copy = pltpu.make_async_remote_copy(
                src_ref=source_of(peer),
                dst_ref=target.at[gy],
                send_sem=send_sem.at[k],
                recv_sem=recv_sem.at[k],
                device_id=(gx, peer),
                device_id_type=MESH,
            )
            copy.start()
            copies.append(copy)
        return copies

    def arrived_x(target, send_sem, recv_sem):
        for k in range(1, n_gx):
            place = target.at[lax.rem(gx + n_gx - k, n_gx)]
            pltpu.make_async_remote_copy(
                src_ref=place,
                dst_ref=place,
                send_sem=send_sem.at[k],
                recv_sem=recv_sem.at[k],
                device_id=(along_x(k), gy),
                device_id_type=MESH,
            ).wait_recv()

    def arrived_y(target, send_sem, recv_sem):
        for k in range(1, n_gy):
            place = target.at[lax.rem(gy + n_gy - k, n_gy)]
            pltpu.make_async_remote_copy(
                src_ref=place,
                dst_ref=place,
                send_sem=send_sem.at[k],
                recv_sem=recv_sem.at[k],
                device_id=(gx, along_y(k)),
                device_id_type=MESH,
            ).wait_recv()

    sends = []
    sends += stage_x(
        lambda peer: payload.at[pl.ds(pl.multiple_of(peer * n_gy, n_gy), n_gy)],
        recv_one,
        one_send,
        one_recv,
    )
    recv_one[gx] = payload[pl.ds(pl.multiple_of(gx * n_gy, n_gy), n_gy), :]

    states = (soil_a, soil_b)

    def soil_step(step):
        for chunk in range(CHUNKS):
            advance(step, chunk, states[step % 2], states[(step + 1) % 2])

    for copy in loads[1:4]:
        copy.wait()
    soil_step(0)
    soil_step(1)

    arrived_x(recv_one, one_send, one_recv)
    for q in range(n_gy):
        for s in range(n_gx):
            mid_one[q, pl.ds(s, 1), :] = recv_one[s, pl.ds(q, 1), :]
    sends += stage_y(lambda peer: mid_one.at[peer], request, two_send, two_recv)
    request[gy] = mid_one[gy]

    soil_step(2)
    soil_step(3)

    arrived_y(request, two_send, two_recv)
    for q in range(WIDE // 128):
        request_t[pl.ds(q * 128, 128), :] = (
            request[:, :, pl.ds(q * 128, 128)].reshape(tiles, 128).T
        )
    column_number = lax.broadcasted_iota(jnp.int32, (256, 128), 0).astype(f32)

    def make_hot(d, unused):
        wanted = request_t[pl.ds(COL + d, 1), :]
        hot[:, pl.ds(pl.multiple_of(d * 128, 128), 128)] = (
            (column_number == wanted).astype(f32).astype(bf16)
        )
        return unused

    lax.fori_loop(0, SLOTS, make_hot, 0)

    for step in range(4, STEPS):
        soil_step(step)
    final = states[STEPS % 2]
    stores = [
        pltpu.make_async_copy(final.at[pl.ds(0, cells)], next_hbm, out_sem.at[0]),
        pltpu.make_async_copy(
            states[(STEPS + 1) % 2].at[pl.ds(0, cells)], before_hbm, out_sem.at[1]
        ),
    ]
    for copy in stores:
        copy.start()

    table = jnp.concatenate(split(jnp.concatenate([motion[0], motion[1]], 1)), 1)
    line_number = lax.broadcasted_iota(jnp.int32, (rows, 128), 0).astype(f32)

    def pick(pair, unused):
        cols = pl.ds(pl.multiple_of(pair * 256, 256), 256)
        chosen = hot[:, cols]
        found = nn(table, jnp.concatenate([chosen, chosen], 0))
        for half in range(2):
            d = pair * 2 + half
            wanted = request_t[pl.ds(ROW + d, 1), :]
            total = jnp.zeros((STEPS, 128), f32)
            for r in range(rows):
                total += jnp.where(
                    wanted == float(r),
                    found[r * STEPS : (r + 1) * STEPS, half * 128 : (half + 1) * 128],
                    0.0,
                )
            picked[pl.ds(pl.multiple_of(d * STEPS, STEPS), STEPS), :] = total
        return unused

    lax.fori_loop(0, SLOTS // 2, pick, 0)
    for q in range(2):
        reply[:, :, pl.ds(q * 128, 128)] = (
            picked[pl.ds(q * 128, 128), :].T.reshape(n_gy, n_gx, 128)
        )
    sends += stage_y(lambda peer: reply.at[peer], recv_two, three_send, three_recv)
    recv_two[gy] = reply[gy]

    def land(pair, total):
        cols = pl.ds(pl.multiple_of(pair * 256, 256), 256)
        parts = []
        for half in range(2):
            d = pair * 2 + half
            eight = pl.ds(pl.multiple_of(d * STEPS, STEPS), STEPS)
            mean = request_t[pl.ds(BASE + d, 1), :] + jnp.sum(
                request_t[eight, :] * picked[eight, :], 0, keepdims=True
            )
            parts.append(jnp.where(line_number == request_t[pl.ds(ROW + d, 1), :], mean, 0.0))
        values = jnp.concatenate(parts, 1)
        return total + nt(jnp.concatenate(split(values), 0), hot[:, cols])

    landed = lax.fori_loop(0, SLOTS // 2, land, jnp.zeros((2 * rows, 256), f32))
    base[...] = landed[:rows] + landed[rows:]
    stores.append(pltpu.make_async_copy(base, base_out, out_sem.at[2]))
    stores[-1].start()

    arrived_y(recv_two, three_send, three_recv)
    for s in range(n_gx):
        for q in range(n_gy):
            mid_two[s, pl.ds(q, 1), :] = recv_two[q, pl.ds(s, 1), :]
    sends += stage_x(lambda peer: mid_two.at[peer], answer, four_send, four_recv)
    answer[gx] = mid_two[gx]
    arrived_x(answer, four_send, four_recv)

    answer_t = jnp.concatenate(
        [answer[:, :, pl.ds(q * 128, 128)].reshape(tiles, 128).T for q in range(2)], 0
    )
    decoded = jnp.concatenate(split(answer_t), 1)
    level = lax.broadcasted_iota(jnp.int32, (32, BLOCK), 0)

    def window(j, unused):
        cols = pl.ds(pl.multiple_of(j * BLOCK, BLOCK), BLOCK)
        mark = marks[:, cols]
        found = nn(decoded, jnp.concatenate([mark, mark], 0))
        rank = rank_ref[:, cols]
        ground = jnp.zeros((STEPS, BLOCK), f32)
        for d in range(SLOTS):
            ground += jnp.where(rank == d, found[d * STEPS : (d + 1) * STEPS], 0.0)
        k, place, speed = stiff[:, cols], disp[:, cols], vel[:, cols]
        for step in range(STEPS):
            beneath = jnp.where(level == 0, ground[step : step + 1], pltpu.roll(place, 1, 0))
            shear = k * (place - beneath)
            upper = jnp.where(level == 31, 0.0, pltpu.roll(shear, 31, 0))
            speed = speed + upper - shear
            place = place + speed
        disp_new[:, cols] = place
        vel_new[:, cols] = speed
        return unused

    lax.fori_loop(0, count // BLOCK, window, 0)
    stores.append(pltpu.make_async_copy(disp_new, disp_out, out_sem.at[3]))
    stores.append(pltpu.make_async_copy(vel_new, vel_out, out_sem.at[4]))
    for copy in stores[3:]:
        copy.start()
    for copy in sends:
        copy.wait_send()
    for slot in range(STEPS):
        for chunk in range(CHUNKS):
            for side in range(4):

                @pl.when(has[side])
                def _():
                    halo(slot, chunk, side).wait_send()

    for copy in stores:
        copy.wait()


def shards(
    soil_now,
    soil_old,
    kappa,
    force_prev,
    storey_disp,
    storey_vel,
    stiffness,
    branch_flag,
    footprint_tile,
    footprint_cell,
):
    n_gx, n_gy = lax.axis_size("gx"), lax.axis_size("gy")
    depth, rows, wide = soil_now.shape
    storeys, count = storey_disp.shape
    tiles = n_gx * n_gy
    flat = (depth * rows, wide)
    any_space = pl.BlockSpec(memory_space=pl.ANY)
    dma = pltpu.SemaphoreType.DMA
    vm = pltpu.VMEM
    out = pl.pallas_call(
        functools.partial(kernel, n_gx, n_gy, depth, rows),
        out_shape=(
            jax.ShapeDtypeStruct(flat, f32),
            jax.ShapeDtypeStruct(flat, f32),
            jax.ShapeDtypeStruct((storeys, count), f32),
            jax.ShapeDtypeStruct((storeys, count), f32),
            jax.ShapeDtypeStruct((rows, wide), f32),
        ),
        in_specs=[pl.BlockSpec(memory_space=pltpu.VMEM)] * 2 + [any_space] * 8,
        out_specs=(any_space,) * 5,
        scratch_shapes=[
            vm((flat[0] + rows, wide), f32),
            vm((flat[0] + rows, wide), f32),
            vm(flat, f32),
            vm((rows, wide), f32),
            vm((storeys, count), f32),
            vm((storeys, count), f32),
            vm((storeys, count), f32),
            vm((storeys, count), jnp.int32),
            vm((storeys, count), f32),
            vm((storeys, count), f32),
            vm((rows, wide), f32),
            vm((STEPS, 2, 2, depth, 128), f32),
            vm((STEPS, 2, 2, depth, 128), f32),
            vm((STEPS, CHUNKS, 2, rows, 128), f32),
            vm((STEPS, CHUNKS, 2, rows, 128), f32),
            vm((tiles, count), bf16),
            vm((1, count), jnp.int32),
            vm((tiles, WIDE), f32),
            vm((n_gx, n_gy, WIDE), f32),
            vm((n_gy, n_gx, WIDE), f32),
            vm((n_gy, n_gx, WIDE), f32),
            vm((WIDE, tiles), f32),
            vm((wide, SLOTS * tiles), bf16),
            vm((2, rows * STEPS, 128), f32),
            vm((SLOTS * STEPS, tiles), f32),
            vm((n_gy, n_gx, SLOTS * STEPS), f32),
            vm((n_gy, n_gx, SLOTS * STEPS), f32),
            vm((n_gx, n_gy, SLOTS * STEPS), f32),
            vm((n_gx, n_gy, SLOTS * STEPS), f32),
            dma((8,)),
            dma((5,)),
            dma((STEPS, CHUNKS, 4)),
            dma((STEPS, CHUNKS, 4)),
            dma((n_gx,)),
            dma((n_gx,)),
            dma((n_gy,)),
            dma((n_gy,)),
            dma((n_gy,)),
            dma((n_gy,)),
            dma((n_gx,)),
            dma((n_gx,)),
        ],
        compiler_params=pltpu.CompilerParams(
            collective_id=0, has_side_effects=True, vmem_limit_bytes=40 * 1024 * 1024
        ),
        cost_estimate=pl.CostEstimate(
            flops=4_000_000_000, bytes_accessed=10_000_000, transcendentals=0
        ),
    )(
        footprint_tile.reshape(1, count),
        footprint_cell.reshape(1, count),
        soil_now.reshape(flat),
        soil_old.reshape(flat),
        kappa.reshape(flat),
        force_prev,
        storey_disp,
        storey_vel,
        stiffness,
        branch_flag,
    )
    return (
        out[0].reshape(soil_now.shape),
        out[1].reshape(soil_now.shape),
        out[2],
        out[3],
        out[4],
    )


def solution(mesh):
    return jax.shard_map(
        shards,
        mesh=mesh,
        in_specs=(
            P(None, "gx", "gy"),
            P(None, "gx", "gy"),
            P(None, "gx", "gy"),
            P("gx", "gy"),
            P(None, ("gx", "gy")),
            P(None, ("gx", "gy")),
            P(None, ("gx", "gy")),
            P(None, ("gx", "gy")),
            P(("gx", "gy"), None),
            P(("gx", "gy")),
        ),
        out_specs=(
            P(None, "gx", "gy"),
            P(None, "gx", "gy"),
            P(None, ("gx", "gy")),
            P(None, ("gx", "gy")),
            P("gx", "gy"),
        ),
        check_vma=False,
    )
```

profile of v0, /device:TPU:1, one launch (start us, length us, event | category | flops | bytes accessed | tf_op | source)
XLA Modules:
  0.0 112.9 jit_solution(6437890661372956798)
XLA Ops:
  0.6 0.0 copy-start
  0.6 1.4 %copy-done = f32[48,32,256]{2,1,0:T(8,128)S(1)} copy-done((f32[48,32,256]{2,1,0:T(8,128)S(1)}, f32[48,32,256]{2,1,0:T(8,128)}, u32[]{:S(2)}) %copy-start) | copy-done | bytes 1572888
  2.0 0.0 copy-start.1
  2.0 1.4 %copy-done.1 = f32[48,32,256]{2,1,0:T(8,128)S(1)} copy-done((f32[48,32,256]{2,1,0:T(8,128)S(1)}, f32[48,32,256]{2,1,0:T(8,128)}, u32[]{:S(2)}) %copy-start.1) | copy-done | bytes 1572888
  3.5 0.0 copy-start.2
  3.5 1.4 %copy-done.2 = f32[48,32,256]{2,1,0:T(8,128)S(1)} copy-done((f32[48,32,256]{2,1,0:T(8,128)S(1)}, f32[48,32,256]{2,1,0:T(8,128)}, u32[]{:S(2)}) %copy-start.2) | copy-done | bytes 1572888
  4.9 0.0 copy-start.3
  4.9 0.9 copy-done.3
  5.8 0.0 copy-start.4
  5.8 0.9 copy-done.4
  6.8 0.0 copy-start.5
  6.8 0.9 copy-done.5
  7.7 0.0 copy-start.6
  7.7 0.9 copy-done.6
  8.7 0.0 copy-start.7
  8.7 0.8 copy-done.7
  9.4 0.0 copy-start.8
  9.4 0.7 copy-done.8
  10.1 0.0 copy-start.9
  10.1 0.7 copy-done.9
  10.8 97.8 %shard_map.137 = (f32[1536,256]{1,0:T(8,128)S(1)}, f32[1536,256]{1,0:T(8,128)S(1)}, f32[32,2048]{1,0:T(8,128)S(1)}, f32[32,2048]{1,0:T(8,128)S(1)}, f32[32,256]{1,0:T(8,128)S(1)}) custom-call(s32[1,2048]{1,0:T(1,128)S(1)} %bitcast.12, s32[1,2048]{1,0:T(1,128)S(1)} %bitcast.13, f32[1536,256]{1,0:T(8,128)S(1)} %bitcast.9, f32[1536,256]{1,0:T(8,128)S(1)} %bitcast.10, ...), custom_call_target="tpu_custom_call" | custom-call | flops 4000000000 | bytes 10000000 | tf_op jit(solution)/shard_map/pallas_call | solution.py:569
  108.6 1.1 %copy.20 = f32[48,32,256]{2,1,0:T(8,128)} copy(f32[48,32,256]{2,1,0:T(8,128)S(1)} %bitcast.8) | data formatting | bytes 3145728
  109.8 1.1 %copy.21 = f32[48,32,256]{2,1,0:T(8,128)} copy(f32[48,32,256]{2,1,0:T(8,128)S(1)} %bitcast.7) | data formatting | bytes 3145728
  110.9 0.7 copy.22
  111.6 0.7 copy.23
  112.3 0.6 copy.24
Async XLA Ops:
  0.6 1.4 %copy-start = (f32[48,32,256]{2,1,0:T(8,128)S(1)}, f32[48,32,256]{2,1,0:T(8,128)}, u32[]{:S(2)}) copy-start(f32[48,32,256]{2,1,0:T(8,128)} %param.10) | copy-start | bytes 4718596
  2.0 1.4 %copy-start.1 = (f32[48,32,256]{2,1,0:T(8,128)S(1)}, f32[48,32,256]{2,1,0:T(8,128)}, u32[]{:S(2)}) copy-start(f32[48,32,256]{2,1,0:T(8,128)} %param.11) | copy-start | bytes 4718596
  3.5 1.4 %copy-start.2 = (f32[48,32,256]{2,1,0:T(8,128)S(1)}, f32[48,32,256]{2,1,0:T(8,128)}, u32[]{:S(2)}) copy-start(f32[48,32,256]{2,1,0:T(8,128)} %param.12) | copy-start | bytes 4718596
  4.9 0.9 copy-start.3
  5.8 0.9 copy-start.4
  6.8 0.9 copy-start.5
  7.7 0.9 copy-start.6
  8.7 0.8 copy-start.7
  9.4 0.7 copy-start.8
  10.1 0.7 copy-start.9
where the time goes:
time: 113 us
  Pallas kernels  97.8 us (87%)
  local copies, waits for them, and re-layouts  14.5 us (13%)
    pallas_call x1, Pallas kernels, shards(): pl.pallas_call(functools.partial(kernel, n_gx, n_gy, depth, rows), out_sh...  97.8 us
    unnamed x25, local copies, waits for them, and re-layouts  14.5 us

commit v1 on v0

--- a/solution.py
+++ b/solution.py
@@ -10,7 +10,8 @@
 STEPS = 8
 force_gain = 0.05
 f32, bf16 = jnp.float32, jnp.bfloat16
-CHUNKS = 2
+GROUP = 4
+PAD = 8
 SLOTS = 32
 COEF, BASE, ROW, COL, WIDE = 0, 256, 288, 320, 384
 BLOCK = 256
@@ -63,6 +64,8 @@
     base,
     x_send,
     x_recv,
+    x_send_top,
+    x_recv_top,
     y_send,
     y_recv,
     marks,
@@ -95,20 +98,20 @@
     gx, gy = lax.axis_index("gx"), lax.axis_index("gy")
     tiles = n_gx * n_gy
     count = tile_ref.shape[1]
-    planes = depth // CHUNKS
     cells = depth * rows
 
     loads = []
-    pairs = (
-        (now_hbm, soil_a.at[pl.ds(0, cells)]),
-        (old_hbm, soil_b.at[pl.ds(0, cells)]),
-        (kappa_hbm, kappa),
+    pairs = []
+    for source, target in ((now_hbm, soil_a), (old_hbm, soil_b), (kappa_hbm, kappa)):
+        for i in range(2):
+            pairs.append((source.at[:, pl.ds(i * 128, 128)], target.at[i, pl.ds(PAD, cells)]))
+    pairs += [
         (force_hbm, force),
         (disp_hbm, disp),
         (vel_hbm, vel),
         (stiff_hbm, stiff),
         (flag_hbm, flag),
-    )
+    ]
     for i, (source, target) in enumerate(pairs):
         copy = pltpu.make_async_copy(source, target, in_sem.at[i])
         copy.start()
@@ -124,8 +127,8 @@
             barrier, inc=1, device_id=(gx, lax.rem(gy + k, n_gy)), device_id_type=MESH
         )
 
-    soil_a[pl.ds(cells, rows), :] = jnp.zeros((rows, 256), f32)
-    soil_b[pl.ds(cells, rows), :] = jnp.zeros((rows, 256), f32)
+    for ref in (soil_a, soil_b):
+        ref[:, pl.ds(PAD + cells, rows), :] = jnp.zeros((2, rows, 128), f32)
     has = (gx > 0, gx < n_gx - 1, gy > 0, gy < n_gy - 1)
     for side in range(4):
 
@@ -133,147 +136,179 @@
         def _():
             if side < 2:
                 x_recv[:, side] = jnp.zeros((STEPS, 2, depth, 128), f32)
+                x_recv_top[:, side] = jnp.zeros((STEPS, 2, STEPS, 128), f32)
             else:
-                y_recv[:, :, side - 2] = jnp.zeros((STEPS, CHUNKS, rows, 128), f32)
+                y_recv[:, :, side - 2] = jnp.zeros((STEPS, 2, rows, 128), f32)
 
     neighbour = ((gx - 1, gy), (gx + 1, gy), (gx, gy - 1), (gx, gy + 1))
 
-    def halo(slot, chunk, side):
-        other = side ^ 1
+    def halo(slot, part, side, arriving=False):
+        place = side if arriving else side ^ 1
         if side < 2:
-            source = x_send.at[slot, side, :, pl.ds(chunk * planes, planes)]
-            target = x_recv.at[slot, other, :, pl.ds(chunk * planes, planes)]
+            outgoing, incoming = (x_send_top, x_recv_top) if part == 0 else (x_send, x_recv)
+            source, target = outgoing.at[slot, side], incoming.at[slot, place]
         else:
-            source = y_send.at[slot, chunk, side - 2]
-            target = y_recv.at[slot, chunk, other - 2]
+            source, target = y_send.at[slot, part, side - 2], y_recv.at[slot, part, place - 2]
         return pltpu.make_async_remote_copy(
             src_ref=source,
             dst_ref=target,
-            send_sem=halo_send.at[slot, chunk, side],
-            recv_sem=halo_recv.at[slot, chunk, other],
+            send_sem=halo_send.at[slot, part, side],
+            recv_sem=halo_recv.at[slot, part, place],
             device_id=neighbour[side],
             device_id_type=MESH,
         )
 
-    def arrival(slot, chunk, side):
-        if side < 2:
-            target = x_recv.at[slot, side, :, pl.ds(chunk * planes, planes)]
-        else:
-            target = y_recv.at[slot, chunk, side - 2]
-        return pltpu.make_async_remote_copy(
-            src_ref=target,
-            dst_ref=target,
-            send_sem=halo_send.at[slot, chunk, side],
-            recv_sem=halo_recv.at[slot, chunk, side],
-            device_id=neighbour[side],
-            device_id_type=MESH,
-        )
-
-    def send_halo(slot, chunk):
+    def send_halo(slot, part):
         for side in range(4):
 
             @pl.when(has[side])
             def _():
-                halo(slot, chunk, side).start()
-
-    def wait_halo(slot, chunk):
+                halo(slot, part, side).start()
+
+    def wait_halo(slot, part):
         for side in range(4):
 
             @pl.when(has[side])
             def _():
-                arrival(slot, chunk, side).wait_recv()
-
-    def edge_rows(slot, z, i, value):
-        x_send[slot, 0, i, pl.ds(z, 1), :] = value[0:1]
-        x_send[slot, 1, i, pl.ds(z, 1), :] = value[rows - 1 : rows]
+                halo(slot, part, side, True).wait_recv()
 
     lane = lax.broadcasted_iota(jnp.int32, (rows, 128), 1)
-    line = lax.broadcasted_iota(jnp.int32, (rows, 128), 0)
+    first_lane, last_lane = lane == 0, lane == 127
+    eight = lax.broadcasted_iota(jnp.int32, (8, 128), 0)
+    no_edges = (jnp.zeros((rows, 128), f32), jnp.zeros((rows, 128), f32))
+
+    def edge_rows(slot, part, z, i, value):
+        ref = x_send_top if part == 0 else x_send
+        ref[slot, 0, i, pl.ds(z, 1), :] = value[0:1]
+        ref[slot, 1, i, pl.ds(z, 1), :] = value[rows - 1 : rows]
 
     def pack(edges, z, low, high):
+        here = lane == z
         return (
-            jnp.where(lane == z, jnp.broadcast_to(low[:, 0:1], (rows, 128)), edges[0]),
-            jnp.where(lane == z, jnp.broadcast_to(high[:, 127:128], (rows, 128)), edges[1]),
-        )
-
-    def plane(z):
-        return pl.ds(pl.multiple_of(z * rows, rows), rows)
-
-    def advance_plane(slot, chunk, here, there, z, edges, top):
-        above_z = 0 if top else z - 1
-        fresh = []
-        halves = [here[plane(z), 0:128], here[plane(z), 128:256]]
-        turned = [pltpu.roll(half, 1, 1) for half in halves]
-        back = [pltpu.roll(half, 127, 1) for half in halves]
-        west = pltpu.roll(y_recv[slot, chunk, 0], 128 - z, 1)
-        east = pltpu.roll(y_recv[slot, chunk, 1], 127 - z, 1)
-        lows = [jnp.where(lane == 0, west, turned[0]), jnp.where(lane == 0, turned[0], turned[1])]
-        highs = [jnp.where(lane == 127, back[1], back[0]), jnp.where(lane == 127, east, back[1])]
-        for i in range(2):
-            cols = pl.ds(i * 128, 128)
-            centre = halves[i]
-            north = jnp.where(
-                line == 0, x_recv[slot, 0, i, pl.ds(z, 1), :], pltpu.roll(centre, 1, 0)
+            jnp.where(here, jnp.broadcast_to(low[:, 0:1], (rows, 128)), edges[0]),
+            jnp.where(here, jnp.broadcast_to(high[:, 127:128], (rows, 128)), edges[1]),
+        )
+
+    def keep_edges(slot, part, edges):
+        y_send[slot, part, 0] = edges[0]
+        y_send[slot, part, 1] = edges[1]
+
+    def plane(z, shift=0):
+        return pl.ds(PAD + z * rows + shift, rows)
+
+    def aligned(z):
+        return pl.ds(pl.multiple_of(PAD + z * rows, 8), rows)
+
+    def advance_planes(step, out_part, in_part, here, there, layers, edges, west, east):
+        incoming = x_recv_top if in_part == 0 else x_recv
+        results = []
+        for z, top in layers:
+            fresh = []
+            halves = [here[0, aligned(z), :], here[1, aligned(z), :]]
+            turned = [pltpu.roll(half, 1, 1) for half in halves]
+            back = [pltpu.roll(half, 127, 1) for half in halves]
+            low = pltpu.roll(west, 128 - z, 1)
+            high = pltpu.roll(east, 127 - z, 1)
+            lows = [jnp.where(first_lane, low, turned[0]), jnp.where(first_lane, turned[0], turned[1])]
+            highs = [jnp.where(last_lane, back[1], back[0]), jnp.where(last_lane, high, back[1])]
+            for i in range(2):
+                centre = halves[i]
+                north = here[i, plane(z, -1), :]
+                south = here[i, plane(z, 1), :]
+                north = jnp.concatenate(
+                    [jnp.where(eight == 0, incoming[step, 0, i, pl.ds(z, 1), :], north[0:8]), north[8:]],
+                    0,
+                )
+                south = jnp.concatenate(
+                    [
+                        south[: rows - 8],
+                        jnp.where(
+                            eight == 7, incoming[step, 1, i, pl.ds(z, 1), :], south[rows - 8 :]
+                        ),
+                    ],
+                    0,
+                )
+                above = centre if top else here[i, aligned(z - 1), :]
+                below = here[i, aligned(z + 1), :]
+                spread = (north + south) + (lows[i] + highs[i]) + (above + below) - 6.0 * centre
+                value = (
+                    2.0 * centre - there[i, aligned(z), :] + kappa[i, aligned(z), :] * spread
+                )
+                if top:
+                    value = value + force_gain * force[:, i * 128 : (i + 1) * 128]
+                    motion[i, pl.ds(step, rows, stride=STEPS), :] = value
+                fresh.append(value)
+            results.append(fresh)
+        for (z, top), fresh in zip(layers, results):
+            for i in range(2):
+                there[i, aligned(z), :] = fresh[i]
+                if step < STEPS - 1:
+                    edge_rows(step + 1, out_part, z, i, fresh[i])
+            edges = pack(edges, z, fresh[0], fresh[1])
+        return edges
+
+    states = (soil_a, soil_b)
+
+    def shallow(step):
+        here, there = states[step % 2], states[(step + 1) % 2]
+        wait_halo(step, 0)
+        west, east = y_recv[step, 0, 0], y_recv[step, 0, 1]
+        edges = no_edges
+        for first in range(0, STEPS - step, GROUP):
+            layers = [(z, z == 0) for z in range(first, min(first + GROUP, STEPS - step))]
+            edges = advance_planes(step, 0, 0, here, there, layers, edges, west, east)
+        if step < STEPS - 1:
+            keep_edges(step + 1, 0, edges)
+            send_halo(step + 1, 0)
+
+    def deep(step):
+        here, there = states[step % 2], states[(step + 1) % 2]
+        wait_halo(step, 1)
+        edges, first = no_edges, STEPS - step
+        if step > 0:
+            edges = advance_planes(
+                step, 1, 0, here, there, [(first, False)], edges, y_recv[step, 0, 0], y_recv[step, 0, 1]
             )
-            south = jnp.where(
-                line == rows - 1,
-                x_recv[slot, 1, i, pl.ds(z, 1), :],
-                pltpu.roll(centre, rows - 1, 0),
-            )
-            above = here[plane(above_z), cols]
-            below = here[plane(z + 1), cols]
-            spread = (north + south) + (lows[i] + highs[i]) + (above + below) - 6.0 * centre
-            value = 2.0 * centre - there[plane(z), cols] + kappa[plane(z), cols] * spread
-            if top:
-                value = value + force_gain * force[:, cols]
-            there[plane(z), cols] = value
-            if slot < STEPS - 1:
-                edge_rows(slot + 1, z, i, value)
-            fresh.append(value)
-            if top:
-                motion[i, pl.ds(slot, rows, stride=STEPS), :] = value
-        return pack(edges, z, fresh[0], fresh[1])
-
-    def advance(step, chunk, here, there):
-        wait_halo(step, chunk)
-        first = chunk * planes
-        edges = (jnp.zeros((rows, 128), f32), jnp.zeros((rows, 128), f32))
-        if chunk == 0:
-            edges = advance_plane(step, chunk, here, there, 0, edges, True)
-        edges = lax.fori_loop(
-            max(first, 1),
-            first + planes,
-            lambda z, kept: advance_plane(step, chunk, here, there, z, kept, False),
-            edges,
-        )
+            first += 1
+        west, east = y_recv[step, 1, 0], y_recv[step, 1, 1]
+        spare = (depth - first) % GROUP
+        if spare:
+            layers = [(z, False) for z in range(first, first + spare)]
+            edges = advance_planes(step, 1, 1, here, there, layers, edges, west, east)
+            first += spare
+
+        def some(g, kept):
+            z = first + g * GROUP
+            layers = [(z + i, False) for i in range(GROUP)]
+            return advance_planes(step, 1, 1, here, there, layers, kept, west, east)
+
+        edges = lax.fori_loop(0, (depth - first) // GROUP, some, edges)
         if step < STEPS - 1:
-            y_send[step + 1, chunk, 0] = edges[0]
-            y_send[step + 1, chunk, 1] = edges[1]
-            send_halo(step + 1, chunk)
-
-    loads[0].wait()
-    for chunk in range(CHUNKS):
-        first = chunk * planes
-
-        def first_edges(z, kept):
-            low, high = soil_a[plane(z), 0:128], soil_a[plane(z), 128:256]
-            edge_rows(0, z, 0, low)
-            edge_rows(0, z, 1, high)
-            return pack(kept, z, low, high)
-
-        edges = lax.fori_loop(
-            first,
-            first + planes,
-            first_edges,
-            (jnp.zeros((rows, 128), f32), jnp.zeros((rows, 128), f32)),
-        )
-        y_send[0, chunk, 0] = edges[0]
-        y_send[0, chunk, 1] = edges[1]
+            keep_edges(step + 1, 1, edges)
+            send_halo(step + 1, 1)
+
+    for copy in loads[0:2]:
+        copy.wait()
+
+    def first_edges(part):
+        def some(g, kept):
+            for i in range(8):
+                z = g * 8 + i
+                low, high = soil_a[0, aligned(z), :], soil_a[1, aligned(z), :]
+                edge_rows(0, part, z, 0, low)
+                edge_rows(0, part, z, 1, high)
+                kept = pack(kept, z, low, high)
+            return kept
+
+        return some
+
+    keep_edges(0, 0, first_edges(0)(0, no_edges))
+    keep_edges(0, 1, lax.fori_loop(1, depth // 8, first_edges(1), no_edges))
     pl.semaphore_wait(barrier, n_gx + n_gy - 2)
-    for chunk in range(CHUNKS):
-        send_halo(0, chunk)
-
-    for copy in loads[4:]:
+    send_halo(0, 0)
+    send_halo(0, 1)
+
+    for copy in loads[7:]:
         copy.wait()
     stiff[...] = stiff[...] * jnp.where(
         flag[...] == 0, 1.0, jnp.where(flag[...] == 1, 0.6, 0.15)
@@ -399,16 +434,12 @@
     )
     recv_one[gx] = payload[pl.ds(pl.multiple_of(gx * n_gy, n_gy), n_gy), :]
 
-    states = (soil_a, soil_b)
-
-    def soil_step(step):
-        for chunk in range(CHUNKS):
-            advance(step, chunk, states[step % 2], states[(step + 1) % 2])
-
-    for copy in loads[1:4]:
+    for copy in loads[2:7]:
         copy.wait()
-    soil_step(0)
-    soil_step(1)
+    shallow(0)
+    deep(0)
+    shallow(1)
+    deep(1)
 
     arrived_x(recv_one, one_send, one_recv)
     for q in range(n_gy):
@@ -417,8 +448,10 @@
     sends += stage_y(lambda peer: mid_one.at[peer], request, two_send, two_recv)
     request[gy] = mid_one[gy]
 
-    soil_step(2)
-    soil_step(3)
+    shallow(2)
+    deep(2)
+    shallow(3)
+    deep(3)
 
     arrived_y(request, two_send, two_recv)
     for q in range(WIDE // 128):
@@ -436,17 +469,10 @@
 
     lax.fori_loop(0, SLOTS, make_hot, 0)
 
-    for step in range(4, STEPS):
-        soil_step(step)
-    final = states[STEPS % 2]
-    stores = [
-        pltpu.make_async_copy(final.at[pl.ds(0, cells)], next_hbm, out_sem.at[0]),
-        pltpu.make_async_copy(
-            states[(STEPS + 1) % 2].at[pl.ds(0, cells)], before_hbm, out_sem.at[1]
-        ),
-    ]
-    for copy in stores:
-        copy.start()
+    for step in range(4, STEPS - 1):
+        shallow(step)
+        deep(step)
+    shallow(STEPS - 1)
 
     table = jnp.concatenate(split(jnp.concatenate([motion[0], motion[1]], 1)), 1)
     line_number = lax.broadcasted_iota(jnp.int32, (rows, 128), 0).astype(f32)
@@ -476,6 +502,19 @@
     sends += stage_y(lambda peer: reply.at[peer], recv_two, three_send, three_recv)
     recv_two[gy] = reply[gy]
 
+    deep(STEPS - 1)
+    stores = []
+    for state, output in ((states[STEPS % 2], next_hbm), (states[(STEPS + 1) % 2], before_hbm)):
+        for i in range(2):
+            stores.append(
+                pltpu.make_async_copy(
+                    state.at[i, pl.ds(PAD, cells)],
+                    output.at[:, pl.ds(i * 128, 128)],
+                    out_sem.at[len(stores)],
+                )
+            )
+            stores[-1].start()
+
     def land(pair, total):
         cols = pl.ds(pl.multiple_of(pair * 256, 256), 256)
         parts = []
@@ -491,7 +530,7 @@
 
     landed = lax.fori_loop(0, SLOTS // 2, land, jnp.zeros((2 * rows, 256), f32))
     base[...] = landed[:rows] + landed[rows:]
-    stores.append(pltpu.make_async_copy(base, base_out, out_sem.at[2]))
+    stores.append(pltpu.make_async_copy(base, base_out, out_sem.at[4]))
     stores[-1].start()
 
     arrived_y(recv_two, three_send, three_recv)
@@ -528,19 +567,19 @@
         return unused
 
     lax.fori_loop(0, count // BLOCK, window, 0)
-    stores.append(pltpu.make_async_copy(disp_new, disp_out, out_sem.at[3]))
-    stores.append(pltpu.make_async_copy(vel_new, vel_out, out_sem.at[4]))
-    for copy in stores[3:]:
+    stores.append(pltpu.make_async_copy(disp_new, disp_out, out_sem.at[5]))
+    stores.append(pltpu.make_async_copy(vel_new, vel_out, out_sem.at[6]))
+    for copy in stores[5:]:
         copy.start()
     for copy in sends:
         copy.wait_send()
     for slot in range(STEPS):
-        for chunk in range(CHUNKS):
+        for part in range(2):
             for side in range(4):
 
                 @pl.when(has[side])
                 def _():
-                    halo(slot, chunk, side).wait_send()
+                    halo(slot, part, side).wait_send()
 
     for copy in stores:
         copy.wait()
@@ -563,7 +602,7 @@
     storeys, count = storey_disp.shape
     tiles = n_gx * n_gy
     flat = (depth * rows, wide)
-    any_space = pl.BlockSpec(memory_space=pl.ANY)
+    hbm = pl.BlockSpec(memory_space=pltpu.HBM)
     dma = pltpu.SemaphoreType.DMA
     vm = pltpu.VMEM
     out = pl.pallas_call(
@@ -575,12 +614,12 @@
             jax.ShapeDtypeStruct((storeys, count), f32),
             jax.ShapeDtypeStruct((rows, wide), f32),
         ),
-        in_specs=[pl.BlockSpec(memory_space=pltpu.VMEM)] * 2 + [any_space] * 8,
-        out_specs=(any_space,) * 5,
+        in_specs=[pl.BlockSpec(memory_space=pltpu.VMEM)] * 2 + [hbm] * 8,
+        out_specs=(hbm,) * 5,
         scratch_shapes=[
-            vm((flat[0] + rows, wide), f32),
-            vm((flat[0] + rows, wide), f32),
-            vm(flat, f32),
+            vm((2, PAD + flat[0] + rows, 128), f32),
+            vm((2, PAD + flat[0] + rows, 128), f32),
+            vm((2, PAD + flat[0], 128), f32),
             vm((rows, wide), f32),
             vm((storeys, count), f32),
             vm((storeys, count), f32),
@@ -591,8 +630,10 @@
             vm((rows, wide), f32),
             vm((STEPS, 2, 2, depth, 128), f32),
             vm((STEPS, 2, 2, depth, 128), f32),
-            vm((STEPS, CHUNKS, 2, rows, 128), f32),
-            vm((STEPS, CHUNKS, 2, rows, 128), f32),
+            vm((STEPS, 2, 2, STEPS, 128), f32),
+            vm((STEPS, 2, 2, STEPS, 128), f32),
+            vm((STEPS, 2, 2, rows, 128), f32),
+            vm((STEPS, 2, 2, rows, 128), f32),
             vm((tiles, count), bf16),
             vm((1, count), jnp.int32),
             vm((tiles, WIDE), f32),
@@ -607,10 +648,10 @@
             vm((n_gy, n_gx, SLOTS * STEPS), f32),
             vm((n_gx, n_gy, SLOTS * STEPS), f32),
             vm((n_gx, n_gy, SLOTS * STEPS), f32),
-            dma((8,)),
-            dma((5,)),
-            dma((STEPS, CHUNKS, 4)),
-            dma((STEPS, CHUNKS, 4)),
+            dma((11,)),
+            dma((7,)),
+            dma((STEPS, 2, 4)),
+            dma((STEPS, 2, 4)),
             dma((n_gx,)),
             dma((n_gx,)),
             dma((n_gy,)),
@@ -621,7 +662,7 @@
             dma((n_gx,)),
         ],
         compiler_params=pltpu.CompilerParams(
-            collective_id=0, has_side_effects=True, vmem_limit_bytes=40 * 1024 * 1024
+            collective_id=0, has_side_effects=True, vmem_limit_bytes=62 * 1024 * 1024
         ),
         cost_estimate=pl.CostEstimate(
             flops=4_000_000_000, bytes_accessed=10_000_000, transcendentals=0

time: 113 us -> 82.1 us (0.73)
  the two profiles are of different devices: /device:TPU:1 before, /device:TPU:2 now
where the time goes in v1:
time: 82.1 us; the launch traced here: 81.1 us
  Pallas kernels  74.4 us (91%)
  local copies, waits for them, and re-layouts  6.03 us (7%)
    pallas_call x1, Pallas kernels, shards(): pl.pallas_call(functools.partial(kernel, n_gx, n_gy, depth, rows), out_sh...  74.4 us
    unnamed x13, local copies, waits for them, and re-layouts  6.03 us

profile of v1, /device:TPU:2, one launch (start us, length us, event | category | flops | bytes accessed | tf_op | source)
XLA Modules:
  0.0 81.1 jit_solution(5978373053475693120)
XLA Ops:
  0.6 74.4 %shard_map.137 = (f32[1536,256]{1,0:T(8,128)}, f32[1536,256]{1,0:T(8,128)}, f32[32,2048]{1,0:T(8,128)}, f32[32,2048]{1,0:T(8,128)}, f32[32,256]{1,0:T(8,128)}) custom-call(s32[1,2048]{1,0:T(1,128)} %bitcast.12, s32[1,2048]{1,0:T(1,128)} %bitcast.13, f32[1536,256]{1,0:T(8,128)} %bitcast.9, f32[1536,256]{1,0:T(8,128)} %bitcast.10, f32[1536,256]{1,0:T(8,128)} %bitcast.11, ...), custom_call_target="tpu_custom_call" | custom-call | flops 4000000000 | bytes 10000000 | tf_op jit(solution)/shard_map/pallas_call | solution.py:608
  75.1 0.0 copy-start
  75.1 2.8 %copy.20 = f32[48,32,256]{2,1,0:T(8,128)} copy(f32[48,32,256]{2,1,0:T(8,128)} %bitcast.8) | data formatting | bytes 3145728
  77.9 0.0 copy-done
  77.9 0.0 copy-start.2
  77.9 0.0 copy-start.1
  77.9 0.0 copy-start.3
  77.9 1.1 %copy.21 = f32[48,32,256]{2,1,0:T(8,128)} copy(f32[48,32,256]{2,1,0:T(8,128)S(1)} %bitcast.7) | data formatting | bytes 3145728
  79.1 0.0 copy-done.2
  79.1 0.7 copy.22
  79.8 0.0 copy-done.1
  79.8 0.7 copy.23
  80.5 0.0 copy-done.3
  80.5 0.6 copy.24
Async XLA Ops:
  75.1 2.9 %copy-start = (f32[1536,256]{1,0:T(8,128)S(1)}, f32[1536,256]{1,0:T(8,128)}, u32[]{:S(2)}) copy-start(f32[1536,256]{1,0:T(8,128)} %get-tuple-element.11) | copy-start | bytes 4718596
  77.9 1.2 %copy-start.2 = (f32[32,2048]{1,0:T(8,128)S(1)}, f32[32,2048]{1,0:T(8,128)}, u32[]{:S(2)}) copy-start(f32[32,2048]{1,0:T(8,128)} %get-tuple-element.22) | copy-start | bytes 786436
  77.9 1.9 %copy-start.1 = (f32[32,2048]{1,0:T(8,128)S(1)}, f32[32,2048]{1,0:T(8,128)}, u32[]{:S(2)}) copy-start(f32[32,2048]{1,0:T(8,128)} %get-tuple-element.23) | copy-start | bytes 786436
  77.9 2.6 %copy-start.3 = (f32[32,256]{1,0:T(8,128)S(1)}, f32[32,256]{1,0:T(8,128)}, u32[]{:S(2)}) copy-start(f32[32,256]{1,0:T(8,128)} %get-tuple-element.24) | copy-start | bytes 98308

commit v2 on v1

--- a/solution.py
+++ b/solution.py
@@ -12,6 +12,7 @@
 f32, bf16 = jnp.float32, jnp.bfloat16
 GROUP = 4
 PAD = 8
+CHUNKS = 2
 SLOTS = 32
 COEF, BASE, ROW, COL, WIDE = 0, 256, 288, 320, 384
 BLOCK = 256
@@ -41,6 +42,9 @@
     now_hbm,
     old_hbm,
     kappa_hbm,
+    now_deep,
+    old_deep,
+    kappa_deep,
     force_hbm,
     disp_hbm,
     vel_hbm,
@@ -64,10 +68,14 @@
     base,
     x_send,
     x_recv,
-    x_send_top,
-    x_recv_top,
     y_send,
     y_recv,
+    cone_now,
+    cone_old,
+    cone_kappa,
+    cone_force,
+    cone_send,
+    cone_recv,
     marks,
     rank_ref,
     payload,
@@ -86,6 +94,10 @@
     out_sem,
     halo_send,
     halo_recv,
+    cone_x_send,
+    cone_x_recv,
+    cone_y_send,
+    cone_y_recv,
     one_send,
     one_recv,
     two_send,
@@ -101,17 +113,21 @@
     cells = depth * rows
 
     loads = []
-    pairs = []
-    for source, target in ((now_hbm, soil_a), (old_hbm, soil_b), (kappa_hbm, kappa)):
-        for i in range(2):
-            pairs.append((source.at[:, pl.ds(i * 128, 128)], target.at[i, pl.ds(PAD, cells)]))
-    pairs += [
-        (force_hbm, force),
+    main = (pl.ds(STEPS, rows), pl.ds(0, 256))
+    pairs = [
         (disp_hbm, disp),
         (vel_hbm, vel),
         (stiff_hbm, stiff),
         (flag_hbm, flag),
+        (force_hbm, force),
+        (now_deep.at[pl.ds(0, STEPS + 1)], cone_now.at[:, main[0], main[1]]),
+        (old_deep.at[pl.ds(0, STEPS)], cone_old.at[:, main[0], main[1]]),
+        (kappa_deep.at[pl.ds(0, STEPS)], cone_kappa.at[:, main[0], main[1]]),
+        (force_hbm, cone_force.at[main[0], main[1]]),
     ]
+    for source, target in ((now_hbm, soil_a), (old_hbm, soil_b), (kappa_hbm, kappa)):
+        for i in range(2):
+            pairs.append((source.at[:, pl.ds(i * 128, 128)], target.at[i, pl.ds(PAD, cells)]))
     for i, (source, target) in enumerate(pairs):
         copy = pltpu.make_async_copy(source, target, in_sem.at[i])
         copy.start()
@@ -130,25 +146,133 @@
     for ref in (soil_a, soil_b):
         ref[:, pl.ds(PAD + cells, rows), :] = jnp.zeros((2, rows, 128), f32)
     has = (gx > 0, gx < n_gx - 1, gy > 0, gy < n_gy - 1)
+    outside = (pl.ds(0, STEPS), pl.ds(STEPS + rows, STEPS))
     for side in range(4):
 
         @pl.when(jnp.logical_not(has[side]))
         def _():
             if side < 2:
                 x_recv[:, side] = jnp.zeros((STEPS, 2, depth, 128), f32)
-                x_recv_top[:, side] = jnp.zeros((STEPS, 2, STEPS, 128), f32)
+                for ref in (cone_now, cone_old, cone_kappa):
+                    ref[:, outside[side], pl.ds(0, 256)] = jnp.zeros(
+                        (ref.shape[0], STEPS, 256), f32
+                    )
+                cone_force[outside[side], pl.ds(0, 256)] = jnp.zeros((STEPS, 256), f32)
             else:
-                y_recv[:, :, side - 2] = jnp.zeros((STEPS, 2, rows, 128), f32)
+                y_recv[:, :, side - 2] = jnp.zeros((STEPS, CHUNKS, rows, 128), f32)
+                cone_recv[side - 2] = jnp.zeros(cone_recv.shape[1:], f32)
 
     neighbour = ((gx - 1, gy), (gx + 1, gy), (gx, gy - 1), (gx, gy + 1))
+
+    def cone_x(side, arriving=False):
+        copies = []
+        sources = (
+            now_deep.at[pl.ds(0, STEPS + 1)],
+            old_deep.at[pl.ds(0, STEPS)],
+            kappa_deep.at[pl.ds(0, STEPS)],
+        )
+        edge = pl.ds(0, STEPS) if side == 0 else pl.ds(rows - STEPS, STEPS)
+        place = side if arriving else side ^ 1
+        for i, target in enumerate((cone_now, cone_old, cone_kappa, cone_force)):
+            if i < 3:
+                source = sources[i].at[:, edge, :]
+                target = target.at[:, outside[place], pl.ds(0, 256)]
+            else:
+                source = force_hbm.at[edge, :]
+                target = target.at[outside[place], pl.ds(0, 256)]
+            copies.append(
+                pltpu.make_async_remote_copy(
+                    src_ref=source,
+                    dst_ref=target,
+                    send_sem=cone_x_send.at[i, side],
+                    recv_sem=cone_x_recv.at[i, place],
+                    device_id=neighbour[side],
+                    device_id_type=MESH,
+                )
+            )
+        return copies
+
+    def cone_y(side, arriving=False):
+        place = side if arriving else side ^ 1
+        return pltpu.make_async_remote_copy(
+            src_ref=cone_send.at[side],
+            dst_ref=cone_recv.at[place],
+            send_sem=cone_y_send.at[side],
+            recv_sem=cone_y_recv.at[place],
+            device_id=neighbour[2 + side],
+            device_id_type=MESH,
+        )
+
+    around = rows + 2 * STEPS
+    cone_lane = lax.broadcasted_iota(jnp.int32, (around, 128), 1)
+    each = [(cone_now, z) for z in range(STEPS + 1)]
+    each += [(ref, z) for ref in (cone_old, cone_kappa) for z in range(STEPS)]
+    each += [(cone_force, None)]
+    width = 128 // STEPS
+
+    def cone_layer(ref, z, cols):
+        return ref[:, cols] if z is None else ref[z, :, cols]
+
+    def cone_edges():
+        for group in range(2):
+            west = jnp.zeros((around, 128), f32)
+            east = jnp.zeros((around, 128), f32)
+            for slot, (ref, z) in enumerate(each[group * width : (group + 1) * width]):
+                here = (cone_lane // STEPS) == slot
+                low = cone_layer(ref, z, pl.ds(0, 128))
+                high = cone_layer(ref, z, pl.ds(128, 128))
+                low = pltpu.roll(low, slot * STEPS, 1) if slot else low
+                west = jnp.where(here, low, west)
+                high = pltpu.roll(high, (slot + 1) * STEPS, 1) if slot < width - 1 else high
+                east = jnp.where(here, high, east)
+            cone_send[0, group] = west
+            cone_send[1, group] = east
+
+    def cone_sides():
+        for group in range(2):
+            west, east = cone_recv[0, group], cone_recv[1, group]
+            for slot, (ref, z) in enumerate(each[group * width : (group + 1) * width]):
+                low = pltpu.roll(west, 128 - (slot + 1) * STEPS, 1) if slot < width - 1 else west
+                high = pltpu.roll(east, 128 - slot * STEPS, 1) if slot else east
+                value = jnp.where(
+                    cone_lane >= 128 - STEPS, low, jnp.where(cone_lane < STEPS, high, 0.0)
+                )
+                if z is None:
+                    ref[:, pl.ds(256, 128)] = value
+                else:
+                    ref[z, :, pl.ds(256, 128)] = value
+
+    def cone_steps():
+        for step in range(STEPS):
+            here, there = (cone_now, cone_old) if step % 2 == 0 else (cone_old, cone_now)
+            for z in range(STEPS - step):
+                centre = here[z]
+                above = centre if z == 0 else here[z - 1]
+                spread = (
+                    (pltpu.roll(centre, 1, 0) + pltpu.roll(centre, around - 1, 0))
+                    + (pltpu.roll(centre, 1, 1) + pltpu.roll(centre, 383, 1))
+                    + (above + here[z + 1])
+                    - 6.0 * centre
+                )
+                value = 2.0 * centre - there[z] + cone_kappa[z] * spread
+                if z == 0:
+                    value = value + force_gain * cone_force[...]
+                    for i in range(2):
+                        motion[i, pl.ds(step, rows, stride=STEPS), :] = value[
+                            STEPS : STEPS + rows, i * 128 : (i + 1) * 128
+                        ]
+                there[z] = value
+
+    planes = depth // CHUNKS
 
     def halo(slot, part, side, arriving=False):
         place = side if arriving else side ^ 1
         if side < 2:
-            outgoing, incoming = (x_send_top, x_recv_top) if part == 0 else (x_send, x_recv)
-            source, target = outgoing.at[slot, side], incoming.at[slot, place]
+            layers = pl.ds(part * planes, planes)
+            source = x_send.at[slot, side, :, layers]
+            target = x_recv.at[slot, place, :, layers]
         else:
-            source, target = y_send.at[slot, part, side - 2], y_recv.at[slot, part, place - 2]
+            source, target = y_send.at[slot, part], y_recv.at[slot, part, place - 2]
         return pltpu.make_async_remote_copy(
             src_ref=source,
             dst_ref=target,
@@ -174,24 +298,18 @@
 
     lane = lax.broadcasted_iota(jnp.int32, (rows, 128), 1)
     first_lane, last_lane = lane == 0, lane == 127
+    odd_lane = (lane % 2) == 1
+    pair_of = lane // 2
     eight = lax.broadcasted_iota(jnp.int32, (8, 128), 0)
-    no_edges = (jnp.zeros((rows, 128), f32), jnp.zeros((rows, 128), f32))
-
-    def edge_rows(slot, part, z, i, value):
-        ref = x_send_top if part == 0 else x_send
-        ref[slot, 0, i, pl.ds(z, 1), :] = value[0:1]
-        ref[slot, 1, i, pl.ds(z, 1), :] = value[rows - 1 : rows]
+    no_edges = jnp.zeros((rows, 128), f32)
+
+    def edge_rows(slot, z, i, value):
+        x_send[slot, 0, i, pl.ds(z, 1), :] = value[0:1]
+        x_send[slot, 1, i, pl.ds(z, 1), :] = value[rows - 1 : rows]
 
     def pack(edges, z, low, high):
-        here = lane == z
-        return (
-            jnp.where(here, jnp.broadcast_to(low[:, 0:1], (rows, 128)), edges[0]),
-            jnp.where(here, jnp.broadcast_to(high[:, 127:128], (rows, 128)), edges[1]),
-        )
-
-    def keep_edges(slot, part, edges):
-        y_send[slot, part, 0] = edges[0]
-        y_send[slot, part, 1] = edges[1]
+        both = pltpu.roll(jnp.where(first_lane, low, high), 2 * z + 1, 1)
+        return jnp.where(pair_of == z, both, edges)
 
     def plane(z, shift=0):
         return pl.ds(PAD + z * rows + shift, rows)
@@ -199,35 +317,32 @@
     def aligned(z):
         return pl.ds(pl.multiple_of(PAD + z * rows, 8), rows)
 
-    def advance_planes(step, out_part, in_part, here, there, layers, edges, west, east):
-        incoming = x_recv_top if in_part == 0 else x_recv
+    def advance_planes(step, here, there, layers, edges, sides):
         results = []
         for z, top in layers:
             fresh = []
             halves = [here[0, aligned(z), :], here[1, aligned(z), :]]
             turned = [pltpu.roll(half, 1, 1) for half in halves]
             back = [pltpu.roll(half, 127, 1) for half in halves]
-            low = pltpu.roll(west, 128 - z, 1)
-            high = pltpu.roll(east, 127 - z, 1)
-            lows = [jnp.where(first_lane, low, turned[0]), jnp.where(first_lane, turned[0], turned[1])]
-            highs = [jnp.where(last_lane, back[1], back[0]), jnp.where(last_lane, high, back[1])]
+            beside = pltpu.roll(sides, 127 - 2 * z, 1)
+            lows = [
+                jnp.where(first_lane, beside, turned[0]),
+                jnp.where(first_lane, turned[0], turned[1]),
+            ]
+            highs = [
+                jnp.where(last_lane, back[1], back[0]),
+                jnp.where(last_lane, beside, back[1]),
+            ]
             for i in range(2):
                 centre = halves[i]
                 north = here[i, plane(z, -1), :]
                 south = here[i, plane(z, 1), :]
-                north = jnp.concatenate(
-                    [jnp.where(eight == 0, incoming[step, 0, i, pl.ds(z, 1), :], north[0:8]), north[8:]],
-                    0,
+                edge = jnp.where(eight == 0, x_recv[step, 0, i, pl.ds(z, 1), :], north[0:8])
+                north = jnp.concatenate([edge, north[8:]], 0)
+                edge = jnp.where(
+                    eight == 7, x_recv[step, 1, i, pl.ds(z, 1), :], south[rows - 8 :]
                 )
-                south = jnp.concatenate(
-                    [
-                        south[: rows - 8],
-                        jnp.where(
-                            eight == 7, incoming[step, 1, i, pl.ds(z, 1), :], south[rows - 8 :]
-                        ),
-                    ],
-                    0,
-                )
+                south = jnp.concatenate([south[: rows - 8], edge], 0)
                 above = centre if top else here[i, aligned(z - 1), :]
                 below = here[i, aligned(z + 1), :]
                 spread = (north + south) + (lows[i] + highs[i]) + (above + below) - 6.0 * centre
@@ -236,79 +351,73 @@
                 )
                 if top:
                     value = value + force_gain * force[:, i * 128 : (i + 1) * 128]
-                    motion[i, pl.ds(step, rows, stride=STEPS), :] = value
                 fresh.append(value)
             results.append(fresh)
         for (z, top), fresh in zip(layers, results):
             for i in range(2):
                 there[i, aligned(z), :] = fresh[i]
                 if step < STEPS - 1:
-                    edge_rows(step + 1, out_part, z, i, fresh[i])
-            edges = pack(edges, z, fresh[0], fresh[1])
+                    edge_rows(step + 1, z, i, fresh[i])
+            if step < STEPS - 1:
+                edges = pack(edges, z, fresh[0], fresh[1])
         return edges
 
     states = (soil_a, soil_b)
 
-    def shallow(step):
+    def advance(step, part):
         here, there = states[step % 2], states[(step + 1) % 2]
-        wait_halo(step, 0)
-        west, east = y_recv[step, 0, 0], y_recv[step, 0, 1]
+        wait_halo(step, part)
+        first, last = part * planes, (part + 1) * planes
+        sides = jnp.where(
+            odd_lane,
+            pltpu.roll(y_recv[step, part, 0], 1, 1),
+            pltpu.roll(y_recv[step, part, 1], 127, 1),
+        )
         edges = no_edges
-        for first in range(0, STEPS - step, GROUP):
-            layers = [(z, z == 0) for z in range(first, min(first + GROUP, STEPS - step))]
-            edges = advance_planes(step, 0, 0, here, there, layers, edges, west, east)
-        if step < STEPS - 1:
-            keep_edges(step + 1, 0, edges)
-            send_halo(step + 1, 0)
-
-    def deep(step):
-        here, there = states[step % 2], states[(step + 1) % 2]
-        wait_halo(step, 1)
-        edges, first = no_edges, STEPS - step
-        if step > 0:
-            edges = advance_planes(
-                step, 1, 0, here, there, [(first, False)], edges, y_recv[step, 0, 0], y_recv[step, 0, 1]
-            )
-            first += 1
-        west, east = y_recv[step, 1, 0], y_recv[step, 1, 1]
-        spare = (depth - first) % GROUP
-        if spare:
-            layers = [(z, False) for z in range(first, first + spare)]
-            edges = advance_planes(step, 1, 1, here, there, layers, edges, west, east)
-            first += spare
+        if part == 0:
+            layers = [(z, z == 0) for z in range(GROUP)]
+            edges = advance_planes(step, here, there, layers, edges, sides)
+            first = GROUP
 
         def some(g, kept):
             z = first + g * GROUP
             layers = [(z + i, False) for i in range(GROUP)]
-            return advance_planes(step, 1, 1, here, there, layers, kept, west, east)
-
-        edges = lax.fori_loop(0, (depth - first) // GROUP, some, edges)
+            return advance_planes(step, here, there, layers, kept, sides)
+
+        edges = lax.fori_loop(0, (last - first) // GROUP, some, edges)
         if step < STEPS - 1:
-            keep_edges(step + 1, 1, edges)
-            send_halo(step + 1, 1)
-
-    for copy in loads[0:2]:
+            y_send[step + 1, part] = edges
+            send_halo(step + 1, part)
+
+    def soil_step(step):
+        for part in range(CHUNKS):
+            advance(step, part)
+
+    pl.semaphore_wait(barrier, n_gx + n_gy - 2)
+    for side in range(2):
+
+        @pl.when(has[side])
+        def _():
+            for copy in cone_x(side):
+                copy.start()
+
+    for copy in loads[9:11]:
         copy.wait()
-
-    def first_edges(part):
-        def some(g, kept):
+    for part in range(CHUNKS):
+
+        def first_edges(g, kept):
             for i in range(8):
-                z = g * 8 + i
+                z = part * planes + g * 8 + i
                 low, high = soil_a[0, aligned(z), :], soil_a[1, aligned(z), :]
-                edge_rows(0, part, z, 0, low)
-                edge_rows(0, part, z, 1, high)
+                edge_rows(0, z, 0, low)
+                edge_rows(0, z, 1, high)
                 kept = pack(kept, z, low, high)
             return kept
 
-        return some
-
-    keep_edges(0, 0, first_edges(0)(0, no_edges))
-    keep_edges(0, 1, lax.fori_loop(1, depth // 8, first_edges(1), no_edges))
-    pl.semaphore_wait(barrier, n_gx + n_gy - 2)
-    send_halo(0, 0)
-    send_halo(0, 1)
-
-    for copy in loads[7:]:
+        y_send[0, part] = lax.fori_loop(0, planes // 8, first_edges, no_edges)
+        send_halo(0, part)
+
+    for copy in loads[0:4]:
         copy.wait()
     stiff[...] = stiff[...] * jnp.where(
         flag[...] == 0, 1.0, jnp.where(flag[...] == 1, 0.6, 0.15)
@@ -434,12 +543,33 @@
     )
     recv_one[gx] = payload[pl.ds(pl.multiple_of(gx * n_gy, n_gy), n_gy), :]
 
-    for copy in loads[2:7]:
+    for copy in loads[4:9]:
         copy.wait()
-    shallow(0)
-    deep(0)
-    shallow(1)
-    deep(1)
+    for side in range(2):
+
+        @pl.when(has[side])
+        def _():
+            for copy in cone_x(side, True):
+                copy.wait_recv()
+
+    cone_edges()
+    for side in range(2):
+
+        @pl.when(has[2 + side])
+        def _():
+            cone_y(side).start()
+
+    for copy in loads[11:]:
+        copy.wait()
+    soil_step(0)
+    for side in range(2):
+
+        @pl.when(has[2 + side])
+        def _():
+            cone_y(side, True).wait_recv()
+
+    cone_sides()
+    cone_steps()
 
     arrived_x(recv_one, one_send, one_recv)
     for q in range(n_gy):
@@ -448,10 +578,8 @@
     sends += stage_y(lambda peer: mid_one.at[peer], request, two_send, two_recv)
     request[gy] = mid_one[gy]
 
-    shallow(2)
-    deep(2)
-    shallow(3)
-    deep(3)
+    soil_step(1)
+    soil_step(2)
 
     arrived_y(request, two_send, two_recv)
     for q in range(WIDE // 128):
@@ -468,11 +596,6 @@
         return unused
 
     lax.fori_loop(0, SLOTS, make_hot, 0)
-
-    for step in range(4, STEPS - 1):
-        shallow(step)
-        deep(step)
-    shallow(STEPS - 1)
 
     table = jnp.concatenate(split(jnp.concatenate([motion[0], motion[1]], 1)), 1)
     line_number = lax.broadcasted_iota(jnp.int32, (rows, 128), 0).astype(f32)
@@ -502,18 +625,8 @@
     sends += stage_y(lambda peer: reply.at[peer], recv_two, three_send, three_recv)
     recv_two[gy] = reply[gy]
 
-    deep(STEPS - 1)
     stores = []
-    for state, output in ((states[STEPS % 2], next_hbm), (states[(STEPS + 1) % 2], before_hbm)):
-        for i in range(2):
-            stores.append(
-                pltpu.make_async_copy(
-                    state.at[i, pl.ds(PAD, cells)],
-                    output.at[:, pl.ds(i * 128, 128)],
-                    out_sem.at[len(stores)],
-                )
-            )
-            stores[-1].start()
+    soil_step(3)
 
     def land(pair, total):
         cols = pl.ds(pl.multiple_of(pair * 256, 256), 256)
@@ -530,15 +643,18 @@
 
     landed = lax.fori_loop(0, SLOTS // 2, land, jnp.zeros((2 * rows, 256), f32))
     base[...] = landed[:rows] + landed[rows:]
-    stores.append(pltpu.make_async_copy(base, base_out, out_sem.at[4]))
+    stores.append(pltpu.make_async_copy(base, base_out, out_sem.at[0]))
     stores[-1].start()
 
+    soil_step(4)
     arrived_y(recv_two, three_send, three_recv)
     for s in range(n_gx):
         for q in range(n_gy):
             mid_two[s, pl.ds(q, 1), :] = recv_two[q, pl.ds(s, 1), :]
     sends += stage_x(lambda peer: mid_two.at[peer], answer, four_send, four_recv)
     answer[gx] = mid_two[gx]
+    soil_step(5)
+    soil_step(6)
     arrived_x(answer, four_send, four_recv)
 
     answer_t = jnp.concatenate(
@@ -567,14 +683,37 @@
         return unused
 
     lax.fori_loop(0, count // BLOCK, window, 0)
-    stores.append(pltpu.make_async_copy(disp_new, disp_out, out_sem.at[5]))
-    stores.append(pltpu.make_async_copy(vel_new, vel_out, out_sem.at[6]))
-    for copy in stores[5:]:
+    stores.append(pltpu.make_async_copy(disp_new, disp_out, out_sem.at[1]))
+    stores.append(pltpu.make_async_copy(vel_new, vel_out, out_sem.at[2]))
+    for copy in stores[1:]:
         copy.start()
+
+    soil_step(7)
+    for state, output in ((states[STEPS % 2], next_hbm), (states[(STEPS + 1) % 2], before_hbm)):
+        for i in range(2):
+            stores.append(
+                pltpu.make_async_copy(
+                    state.at[i, pl.ds(PAD, cells)],
+                    output.at[:, pl.ds(i * 128, 128)],
+                    out_sem.at[len(stores)],
+                )
+            )
+            stores[-1].start()
+    for side in range(2):
+
+        @pl.when(has[side])
+        def _():
+            for copy in cone_x(side):
+                copy.wait_send()
+
+        @pl.when(has[2 + side])
+        def _():
+            cone_y(side).wait_send()
+
     for copy in sends:
         copy.wait_send()
     for slot in range(STEPS):
-        for part in range(2):
+        for part in range(CHUNKS):
             for side in range(4):
 
                 @pl.when(has[side])
@@ -602,6 +741,7 @@
     storeys, count = storey_disp.shape
     tiles = n_gx * n_gy
     flat = (depth * rows, wide)
+    around = rows + 2 * STEPS
     hbm = pl.BlockSpec(memory_space=pltpu.HBM)
     dma = pltpu.SemaphoreType.DMA
     vm = pltpu.VMEM
@@ -614,7 +754,7 @@
             jax.ShapeDtypeStruct((storeys, count), f32),
             jax.ShapeDtypeStruct((rows, wide), f32),
         ),
-        in_specs=[pl.BlockSpec(memory_space=pltpu.VMEM)] * 2 + [hbm] * 8,
+        in_specs=[pl.BlockSpec(memory_space=pltpu.VMEM)] * 2 + [hbm] * 11,
         out_specs=(hbm,) * 5,
         scratch_shapes=[
             vm((2, PAD + flat[0] + rows, 128), f32),
@@ -630,10 +770,14 @@
             vm((rows, wide), f32),
             vm((STEPS, 2, 2, depth, 128), f32),
             vm((STEPS, 2, 2, depth, 128), f32),
-            vm((STEPS, 2, 2, STEPS, 128), f32),
-            vm((STEPS, 2, 2, STEPS, 128), f32),
-            vm((STEPS, 2, 2, rows, 128), f32),
-            vm((STEPS, 2, 2, rows, 128), f32),
+            vm((STEPS, CHUNKS, rows, 128), f32),
+            vm((STEPS, CHUNKS, 2, rows, 128), f32),
+            vm((STEPS + 1, around, 384), f32),
+            vm((STEPS, around, 384), f32),
+            vm((STEPS, around, 384), f32),
+            vm((around, 384), f32),
+            vm((2, 2, around, 128), f32),
+            vm((2, 2, around, 128), f32),
             vm((tiles, count), bf16),
             vm((1, count), jnp.int32),
             vm((tiles, WIDE), f32),
@@ -648,10 +792,14 @@
             vm((n_gy, n_gx, SLOTS * STEPS), f32),
             vm((n_gx, n_gy, SLOTS * STEPS), f32),
             vm((n_gx, n_gy, SLOTS * STEPS), f32),
-            dma((11,)),
+            dma((15,)),
             dma((7,)),
-            dma((STEPS, 2, 4)),
-            dma((STEPS, 2, 4)),
+            dma((STEPS, CHUNKS, 4)),
+            dma((STEPS, CHUNKS, 4)),
+            dma((4, 2)),
+            dma((4, 2)),
+            dma((2,)),
+            dma((2,)),
             dma((n_gx,)),
             dma((n_gx,)),
             dma((n_gy,)),
@@ -673,6 +821,9 @@
         soil_now.reshape(flat),
         soil_old.reshape(flat),
         kappa.reshape(flat),
+        soil_now,
+        soil_old,
+        kappa,
         force_prev,
         storey_disp,
         storey_vel,

time: 82.1 us -> 66.7 us (0.81)
  Pallas kernels: 74.4 us -> 59.8 us
    pallas_call x1, Pallas kernels: 74.4 us -> 59.8 us  [shards(): pl.pallas_call(functools.partial(kernel, n_gx, n_gy, depth, rows), out_sh...]
where the time goes in v2:
time: 66.7 us; the launch traced here: 66.5 us
  Pallas kernels  59.8 us (90%)
  local copies, waits for them, and re-layouts  6.03 us (9%)
    pallas_call x1, Pallas kernels, shards(): pl.pallas_call(functools.partial(kernel, n_gx, n_gy, depth, rows), out_sh...  59.8 us
    unnamed x13, local copies, waits for them, and re-layouts  6.03 us

profile of v2, /device:TPU:2, one launch (start us, length us, event | category | flops | bytes accessed | tf_op | source)
XLA Modules:
  0.0 66.5 jit_solution(8632376368106234367)
XLA Ops:
  0.6 59.8 %shard_map.137 = (f32[1536,256]{1,0:T(8,128)}, f32[1536,256]{1,0:T(8,128)}, f32[32,2048]{1,0:T(8,128)}, f32[32,2048]{1,0:T(8,128)}, f32[32,256]{1,0:T(8,128)}) custom-call(s32[1,2048]{1,0:T(1,128)} %bitcast.12, s32[1,2048]{1,0:T(1,128)} %bitcast.13, f32[1536,256]{1,0:T(8,128)} %bitcast.9, f32[1536,256]{1,0:T(8,128)} %bitcast.10, f32[1536,256]{1,0:T(8,128)} %bitcast.11, ...), custom_call_target="tpu_custom_call" | custom-call | flops 4000000000 | bytes 10000000 | tf_op jit(solution)/shard_map/pallas_call | solution.py:748
  60.4 0.0 copy-start
  60.4 2.8 %copy.20 = f32[48,32,256]{2,1,0:T(8,128)} copy(f32[48,32,256]{2,1,0:T(8,128)} %bitcast.8) | data formatting | bytes 3145728
  63.3 0.0 copy-done
  63.3 0.0 copy-start.2
  63.3 0.0 copy-start.1
  63.3 0.0 copy-start.3
  63.3 1.1 %copy.21 = f32[48,32,256]{2,1,0:T(8,128)} copy(f32[48,32,256]{2,1,0:T(8,128)S(1)} %bitcast.7) | data formatting | bytes 3145728
  64.5 0.0 copy-done.2
  64.5 0.7 %copy.22 = f32[32,2048]{1,0:T(8,128)} copy(f32[32,2048]{1,0:T(8,128)S(1)} %copy-done.2) | data formatting | bytes 524288
  65.2 0.0 copy-done.1
  65.2 0.7 %copy.23 = f32[32,2048]{1,0:T(8,128)} copy(f32[32,2048]{1,0:T(8,128)S(1)} %copy-done.1) | data formatting | bytes 524288
  65.9 0.0 copy-done.3
  65.9 0.6 copy.24
Async XLA Ops:
  60.4 2.9 %copy-start = (f32[1536,256]{1,0:T(8,128)S(1)}, f32[1536,256]{1,0:T(8,128)}, u32[]{:S(2)}) copy-start(f32[1536,256]{1,0:T(8,128)} %get-tuple-element.11) | copy-start | bytes 4718596
  63.3 1.2 %copy-start.2 = (f32[32,2048]{1,0:T(8,128)S(1)}, f32[32,2048]{1,0:T(8,128)}, u32[]{:S(2)}) copy-start(f32[32,2048]{1,0:T(8,128)} %get-tuple-element.22) | copy-start | bytes 786436
  63.3 1.9 %copy-start.1 = (f32[32,2048]{1,0:T(8,128)S(1)}, f32[32,2048]{1,0:T(8,128)}, u32[]{:S(2)}) copy-start(f32[32,2048]{1,0:T(8,128)} %get-tuple-element.23) | copy-start | bytes 786436
  63.3 2.6 %copy-start.3 = (f32[32,256]{1,0:T(8,128)S(1)}, f32[32,256]{1,0:T(8,128)}, u32[]{:S(2)}) copy-start(f32[32,256]{1,0:T(8,128)} %get-tuple-element.24) | copy-start | bytes 98308

commit v3 on v2

--- a/solution.py
+++ b/solution.py
@@ -10,7 +10,7 @@
 STEPS = 8
 force_gain = 0.05
 f32, bf16 = jnp.float32, jnp.bfloat16
-GROUP = 4
+GROUP = 8
 PAD = 8
 CHUNKS = 2
 SLOTS = 32
@@ -586,38 +586,36 @@
         request_t[pl.ds(q * 128, 128), :] = (
             request[:, :, pl.ds(q * 128, 128)].reshape(tiles, 128).T
         )
-    column_number = lax.broadcasted_iota(jnp.int32, (256, 128), 0).astype(f32)
-
-    def make_hot(d, unused):
-        wanted = request_t[pl.ds(COL + d, 1), :]
-        hot[:, pl.ds(pl.multiple_of(d * 128, 128), 128)] = (
-            (column_number == wanted).astype(f32).astype(bf16)
-        )
-        return unused
-
-    lax.fori_loop(0, SLOTS, make_hot, 0)
-
     table = jnp.concatenate(split(jnp.concatenate([motion[0], motion[1]], 1)), 1)
     line_number = lax.broadcasted_iota(jnp.int32, (rows, 128), 0).astype(f32)
 
-    def pick(pair, unused):
-        cols = pl.ds(pl.multiple_of(pair * 256, 256), 256)
-        chosen = hot[:, cols]
+    column_number = lax.broadcasted_iota(jnp.int32, (256, 128), 0).astype(f32)
+    LINES = 4
+
+    def pick(group, unused):
+        chosen = []
+        for i in range(LINES):
+            wanted = request_t[pl.ds(COL + group * LINES + i, 1), :]
+            chosen.append((column_number == wanted).astype(f32).astype(bf16))
+        chosen = jnp.concatenate(chosen, 1)
+        hot[:, pl.ds(pl.multiple_of(group * LINES * 128, 128), LINES * 128)] = chosen
         found = nn(table, jnp.concatenate([chosen, chosen], 0))
-        for half in range(2):
-            d = pair * 2 + half
-            wanted = request_t[pl.ds(ROW + d, 1), :]
-            total = jnp.zeros((STEPS, 128), f32)
+        totals = []
+        for i in range(LINES):
+            wanted = request_t[pl.ds(ROW + group * LINES + i, 1), :]
+            sums = [jnp.zeros((STEPS, 128), f32) for unused_part in range(4)]
             for r in range(rows):
-                total += jnp.where(
+                sums[r % 4] += jnp.where(
                     wanted == float(r),
-                    found[r * STEPS : (r + 1) * STEPS, half * 128 : (half + 1) * 128],
+                    found[r * STEPS : (r + 1) * STEPS, i * 128 : (i + 1) * 128],
                     0.0,
                 )
-            picked[pl.ds(pl.multiple_of(d * STEPS, STEPS), STEPS), :] = total
+            totals.append((sums[0] + sums[1]) + (sums[2] + sums[3]))
+        size = LINES * STEPS
+        picked[pl.ds(pl.multiple_of(group * size, size), size), :] = jnp.concatenate(totals, 0)
         return unused
 
-    lax.fori_loop(0, SLOTS // 2, pick, 0)
+    lax.fori_loop(0, SLOTS // LINES, pick, 0)
     for q in range(2):
         reply[:, :, pl.ds(q * 128, 128)] = (
             picked[pl.ds(q * 128, 128), :].T.reshape(n_gy, n_gx, 128)
@@ -628,20 +626,22 @@
     stores = []
     soil_step(3)
 
-    def land(pair, total):
-        cols = pl.ds(pl.multiple_of(pair * 256, 256), 256)
+    LANDED = 8
+
+    def land(group, total):
+        cols = pl.ds(pl.multiple_of(group * LANDED * 128, 128), LANDED * 128)
         parts = []
-        for half in range(2):
-            d = pair * 2 + half
-            eight = pl.ds(pl.multiple_of(d * STEPS, STEPS), STEPS)
+        for i in range(LANDED):
+            d = group * LANDED + i
+            lines = pl.ds(pl.multiple_of(d * STEPS, STEPS), STEPS)
             mean = request_t[pl.ds(BASE + d, 1), :] + jnp.sum(
-                request_t[eight, :] * picked[eight, :], 0, keepdims=True
+                request_t[lines, :] * picked[lines, :], 0, keepdims=True
             )
             parts.append(jnp.where(line_number == request_t[pl.ds(ROW + d, 1), :], mean, 0.0))
         values = jnp.concatenate(parts, 1)
         return total + nt(jnp.concatenate(split(values), 0), hot[:, cols])
 
-    landed = lax.fori_loop(0, SLOTS // 2, land, jnp.zeros((2 * rows, 256), f32))
+    landed = lax.fori_loop(0, SLOTS // LANDED, land, jnp.zeros((2 * rows, 256), f32))
     base[...] = landed[:rows] + landed[rows:]
     stores.append(pltpu.make_async_copy(base, base_out, out_sem.at[0]))
     stores[-1].start()
@@ -721,6 +721,26 @@
                     halo(slot, part, side).wait_send()
 
     for copy in stores:
+        copy.wait()
+
+
+def hand_over(*refs):
+    sources, targets, held, sems = refs[:5], refs[5:10], refs[10:15], refs[15:]
+    ways = []
+    for source, target, room in zip(sources, targets, held):
+        pieces = 2 if source.shape[0] > 256 else 1
+        size = source.shape[0] // pieces
+        for i in range(pieces):
+            part = pl.ds(i * size, size)
+            ways.append((source.at[part], room.at[part], target.at[part]))
+    reads = [pltpu.make_async_copy(a, b, sems[0].at[i]) for i, (a, b, c) in enumerate(ways)]
+    writes = [pltpu.make_async_copy(b, c, sems[1].at[i]) for i, (a, b, c) in enumerate(ways)]
+    for copy in reads:
+        copy.start()
+    for read, write in zip(reads, writes):
+        read.wait()
+        write.start()
+    for copy in writes:
         copy.wait()
 
 
@@ -830,6 +850,14 @@
         stiffness,
         branch_flag,
     )
+    out = pl.pallas_call(
+        hand_over,
+        out_shape=tuple(jax.ShapeDtypeStruct(a.shape, a.dtype) for a in out),
+        in_specs=[hbm] * 5,
+        out_specs=(hbm,) * 5,
+        scratch_shapes=[vm(a.shape, a.dtype) for a in out] + [dma((7,)), dma((7,))],
+        compiler_params=pltpu.CompilerParams(vmem_limit_bytes=62 * 1024 * 1024),
+    )(*out)
     return (
         out[0].reshape(soil_now.shape),
         out[1].reshape(soil_now.shape),

time: 66.7 us -> 58.8 us (0.88)
  local copies, waits for them, and re-layouts: 6.03 us -> 0 us
  Pallas kernels: 59.8 us -> 58 us
    unnamed x13 -> x0, local copies, waits for them, and re-layouts: 6.03 us -> none
    pallas_call x1, Pallas kernels: 59.8 us -> 54.9 us  [shards(): pl.pallas_call(functools.partial(kernel, n_gx, n_gy, depth, rows), out_sh...]
    pallas_call x0 -> x1, Pallas kernels: none -> 3.08 us  [shards(): pl.pallas_call(hand_over, out_shape=tuple((jax.ShapeDtypeStruct(a.shape,...]
where the time goes in v3:
time: 58.8 us; the launch traced here: 58.6 us
  Pallas kernels  58 us (99%)
  between operations  0.64 us (1%)
    pallas_call x1, Pallas kernels, shards(): pl.pallas_call(functools.partial(kernel, n_gx, n_gy, depth, rows), out_sh...  54.9 us
    pallas_call x1, Pallas kernels, shards(): pl.pallas_call(hand_over, out_shape=tuple((jax.ShapeDtypeStruct(a.shape,...  3.08 us

profile of v3, /device:TPU:2, one launch (start us, length us, event | category | flops | bytes accessed | tf_op | source)
XLA Modules:
  0.0 58.6 jit_solution(16373708908658451316)
XLA Ops:
  0.6 54.9 %shard_map.137 = (f32[1536,256]{1,0:T(8,128)}, f32[1536,256]{1,0:T(8,128)}, f32[32,2048]{1,0:T(8,128)}, f32[32,2048]{1,0:T(8,128)}, f32[32,256]{1,0:T(8,128)}) custom-call(s32[1,2048]{1,0:T(1,128)} %bitcast.12, s32[1,2048]{1,0:T(1,128)} %bitcast.13, f32[1536,256]{1,0:T(8,128)} %bitcast.7, f32[1536,256]{1,0:T(8,128)} %bitcast.8, f32[1536,256]{1,0:T(8,128)} %bitcast.9, ...), custom_call_target="tpu_custom_call" | custom-call | flops 4000000000 | bytes 10000000 | tf_op jit(solution)/shard_map/pallas_call | solution.py:768
  55.5 3.1 %shard_map.138 = (f32[1536,256]{1,0:T(8,128)}, f32[1536,256]{1,0:T(8,128)}, f32[32,2048]{1,0:T(8,128)}, f32[32,2048]{1,0:T(8,128)}, f32[32,256]{1,0:T(8,128)}) custom-call(f32[1536,256]{1,0:T(8,128)} %get-tuple-element.15.refs_0_, f32[1536,256]{1,0:T(8,128)} %get-tuple-element.16.refs_1_, f32[32,2048]{1,0:T(8,128)} %get-tuple-element.17.refs_2_, ...), custom_call_target="tpu_custom_call" | custom-call | tf_op jit(solution)/shard_map/pallas_call | solution.py:853

commit v4 on v3

--- a/solution.py
+++ b/solution.py
@@ -15,7 +15,8 @@
 CHUNKS = 2
 SLOTS = 32
 COEF, BASE, ROW, COL, WIDE = 0, 256, 288, 320, 384
-BLOCK = 256
+BLOCK = 512
+RANKED = 256
 MESH = pl.DeviceIdType.MESH
 
 
@@ -115,6 +116,9 @@
     loads = []
     main = (pl.ds(STEPS, rows), pl.ds(0, 256))
     pairs = [
+        (now_hbm.at[:, pl.ds(i * 128, 128)], soil_a.at[i, pl.ds(PAD, cells)]) for i in range(2)
+    ]
+    pairs += [
         (disp_hbm, disp),
         (vel_hbm, vel),
         (stiff_hbm, stiff),
@@ -125,7 +129,7 @@
         (kappa_deep.at[pl.ds(0, STEPS)], cone_kappa.at[:, main[0], main[1]]),
         (force_hbm, cone_force.at[main[0], main[1]]),
     ]
-    for source, target in ((now_hbm, soil_a), (old_hbm, soil_b), (kappa_hbm, kappa)):
+    for source, target in ((old_hbm, soil_b), (kappa_hbm, kappa)):
         for i in range(2):
             pairs.append((source.at[:, pl.ds(i * 128, 128)], target.at[i, pl.ds(PAD, cells)]))
     for i, (source, target) in enumerate(pairs):
@@ -317,7 +321,7 @@
     def aligned(z):
         return pl.ds(pl.multiple_of(PAD + z * rows, 8), rows)
 
-    def advance_planes(step, here, there, layers, edges, sides):
+    def advance_planes(step, here, there, layers, sides):
         results = []
         for z, top in layers:
             fresh = []
@@ -358,9 +362,6 @@
                 there[i, aligned(z), :] = fresh[i]
                 if step < STEPS - 1:
                     edge_rows(step + 1, z, i, fresh[i])
-            if step < STEPS - 1:
-                edges = pack(edges, z, fresh[0], fresh[1])
-        return edges
 
     states = (soil_a, soil_b)
 
@@ -373,35 +374,36 @@
             pltpu.roll(y_recv[step, part, 0], 1, 1),
             pltpu.roll(y_recv[step, part, 1], 127, 1),
         )
-        edges = no_edges
         if part == 0:
-            layers = [(z, z == 0) for z in range(GROUP)]
-            edges = advance_planes(step, here, there, layers, edges, sides)
+            advance_planes(step, here, there, [(z, z == 0) for z in range(GROUP)], sides)
             first = GROUP
+
+        def behind(z, kept):
+            if step < STEPS - 1:
+                values = [
+                    (z - i, there[0, aligned(z - i), :], there[1, aligned(z - i), :])
+                    for i in range(GROUP, 0, -1)
+                ]
+                for layer, low, high in values:
+                    kept = pack(kept, layer, low, high)
+            return kept
 
         def some(g, kept):
             z = first + g * GROUP
-            layers = [(z + i, False) for i in range(GROUP)]
-            return advance_planes(step, here, there, layers, kept, sides)
-
-        edges = lax.fori_loop(0, (last - first) // GROUP, some, edges)
+            kept = behind(z, kept)
+            advance_planes(step, here, there, [(z + i, False) for i in range(GROUP)], sides)
+            return kept
+
+        edges = lax.fori_loop(0, (last - first) // GROUP, some, no_edges)
         if step < STEPS - 1:
-            y_send[step + 1, part] = edges
+            y_send[step + 1, part] = behind(last, edges)
             send_halo(step + 1, part)
 
     def soil_step(step):
         for part in range(CHUNKS):
             advance(step, part)
 
-    pl.semaphore_wait(barrier, n_gx + n_gy - 2)
-    for side in range(2):
-
-        @pl.when(has[side])
-        def _():
-            for copy in cone_x(side):
-                copy.start()
-
-    for copy in loads[9:11]:
+    for copy in loads[0:2]:
         copy.wait()
     for part in range(CHUNKS):
 
@@ -415,17 +417,25 @@
             return kept
 
         y_send[0, part] = lax.fori_loop(0, planes // 8, first_edges, no_edges)
+    pl.semaphore_wait(barrier, n_gx + n_gy - 2)
+    for part in range(CHUNKS):
         send_halo(0, part)
-
-    for copy in loads[0:4]:
+    for side in range(2):
+
+        @pl.when(has[side])
+        def _():
+            for copy in cone_x(side):
+                copy.start()
+
+    for copy in loads[2:6]:
         copy.wait()
     stiff[...] = stiff[...] * jnp.where(
         flag[...] == 0, 1.0, jnp.where(flag[...] == 1, 0.6, 0.15)
     ).astype(f32)
     payload[...] = jnp.zeros((tiles, WIDE), f32)
     before = (
-        lax.broadcasted_iota(jnp.int32, (BLOCK, BLOCK), 0)
-        < lax.broadcasted_iota(jnp.int32, (BLOCK, BLOCK), 1)
+        lax.broadcasted_iota(jnp.int32, (RANKED, RANKED), 0)
+        < lax.broadcasted_iota(jnp.int32, (RANKED, RANKED), 1)
     ).astype(f32).astype(bf16)
     tile_number = lax.broadcasted_iota(jnp.int32, (tiles, BLOCK), 0)
     slot_number = lax.broadcasted_iota(jnp.int32, (SLOTS, BLOCK), 0)
@@ -436,7 +446,11 @@
         chosen = (tile_number == tile_ref[:, cols]).astype(f32)
         mark = chosen.astype(bf16)
         marks[:, cols] = mark
-        earlier = nn(mark, before) + used
+        earlier = []
+        for i in range(0, BLOCK, RANKED):
+            earlier.append(nn(mark[:, i : i + RANKED], before) + used)
+            used = used + jnp.sum(chosen[:, i : i + RANKED], 1, keepdims=True)
+        earlier = jnp.concatenate(earlier, 1)
         rank = jnp.sum(chosen * earlier, 0, keepdims=True).astype(jnp.int32)
         rank_ref[:, cols] = rank
         k = stiff[0:8, cols]
@@ -468,9 +482,10 @@
         payload[...] += nt(mark, spread_out(coef_high, (constant_high, row, col))) + nt(
             mark, spread_out(coefs - coef_high, (constant - constant_high,))
         )
-        return used + jnp.sum(chosen, 1, keepdims=True)
-
-    lax.fori_loop(0, count // BLOCK, list_block, jnp.zeros((tiles, 1), f32))
+        return used
+
+    blocks = count // BLOCK
+    used = lax.fori_loop(0, blocks // 2, list_block, jnp.zeros((tiles, 1), f32))
 
     def along_x(k):
         return lax.rem(gx + k, n_gx)
@@ -534,6 +549,10 @@
                 device_id_type=MESH,
             ).wait_recv()
 
+    for copy in loads[6:]:
+        copy.wait()
+    soil_step(0)
+    lax.fori_loop(blocks // 2, blocks, list_block, used)
     sends = []
     sends += stage_x(
         lambda peer: payload.at[pl.ds(pl.multiple_of(peer * n_gy, n_gy), n_gy)],
@@ -543,8 +562,6 @@
     )
     recv_one[gx] = payload[pl.ds(pl.multiple_of(gx * n_gy, n_gy), n_gy), :]
 
-    for copy in loads[4:9]:
-        copy.wait()
     for side in range(2):
 
         @pl.when(has[side])
@@ -559,17 +576,7 @@
         def _():
             cone_y(side).start()
 
-    for copy in loads[11:]:
-        copy.wait()
-    soil_step(0)
-    for side in range(2):
-
-        @pl.when(has[2 + side])
-        def _():
-            cone_y(side, True).wait_recv()
-
-    cone_sides()
-    cone_steps()
+    soil_step(1)
 
     arrived_x(recv_one, one_send, one_recv)
     for q in range(n_gy):
@@ -578,8 +585,17 @@
     sends += stage_y(lambda peer: mid_one.at[peer], request, two_send, two_recv)
     request[gy] = mid_one[gy]
 
-    soil_step(1)
     soil_step(2)
+
+    for side in range(2):
+
+        @pl.when(has[2 + side])
+        def _():
+            cone_y(side, True).wait_recv()
+
+    cone_sides()
+    cone_steps()
+    soil_step(3)
 
     arrived_y(request, two_send, two_recv)
     for q in range(WIDE // 128):
@@ -624,7 +640,7 @@
     recv_two[gy] = reply[gy]
 
     stores = []
-    soil_step(3)
+    soil_step(4)
 
     LANDED = 8
 
@@ -646,14 +662,13 @@
     stores.append(pltpu.make_async_copy(base, base_out, out_sem.at[0]))
     stores[-1].start()
 
-    soil_step(4)
+    soil_step(5)
     arrived_y(recv_two, three_send, three_recv)
     for s in range(n_gx):
         for q in range(n_gy):
             mid_two[s, pl.ds(q, 1), :] = recv_two[q, pl.ds(s, 1), :]
     sends += stage_x(lambda peer: mid_two.at[peer], answer, four_send, four_recv)
     answer[gx] = mid_two[gx]
-    soil_step(5)
     soil_step(6)
     arrived_x(answer, four_send, four_recv)
 

time: 58.8 us -> 55.7 us (0.947)
  Pallas kernels: 58 us -> 54.9 us
    pallas_call x1, Pallas kernels: 54.9 us -> 51.8 us  [shards(): pl.pallas_call(functools.partial(kernel, n_gx, n_gy, depth, rows), out_sh...]
where the time goes in v4:
time: 55.7 us; the launch traced here: 55.5 us
  Pallas kernels  54.9 us (99%)
  between operations  0.64 us (1%)
    pallas_call x1, Pallas kernels, shards(): pl.pallas_call(functools.partial(kernel, n_gx, n_gy, depth, rows), out_sh...  51.8 us
    pallas_call x1, Pallas kernels, shards(): pl.pallas_call(hand_over, out_shape=tuple((jax.ShapeDtypeStruct(a.shape,...  3.08 us

profile of v4, /device:TPU:2, one launch (start us, length us, event | category | flops | bytes accessed | tf_op | source)
XLA Modules:
  0.0 55.5 jit_solution(11181072425208253046)
XLA Ops:
  0.6 51.8 %shard_map.137 = (f32[1536,256]{1,0:T(8,128)}, f32[1536,256]{1,0:T(8,128)}, f32[32,2048]{1,0:T(8,128)}, f32[32,2048]{1,0:T(8,128)}, f32[32,256]{1,0:T(8,128)}) custom-call(s32[1,2048]{1,0:T(1,128)} %bitcast.12, s32[1,2048]{1,0:T(1,128)} %bitcast.13, f32[1536,256]{1,0:T(8,128)} %bitcast.7, f32[1536,256]{1,0:T(8,128)} %bitcast.8, f32[1536,256]{1,0:T(8,128)} %bitcast.9, ...), custom_call_target="tpu_custom_call" | custom-call | flops 4000000000 | bytes 10000000 | tf_op jit(solution)/shard_map/pallas_call | solution.py:783
  52.4 3.1 %shard_map.138 = (f32[1536,256]{1,0:T(8,128)}, f32[1536,256]{1,0:T(8,128)}, f32[32,2048]{1,0:T(8,128)}, f32[32,2048]{1,0:T(8,128)}, f32[32,256]{1,0:T(8,128)}) custom-call(f32[1536,256]{1,0:T(8,128)} %get-tuple-element.15.refs_0_, f32[1536,256]{1,0:T(8,128)} %get-tuple-element.16.refs_1_, f32[32,2048]{1,0:T(8,128)} %get-tuple-element.17.refs_2_, ...), custom_call_target="tpu_custom_call" | custom-call | tf_op jit(solution)/shard_map/pallas_call | solution.py:868

commit v5 on v4

--- a/solution.py
+++ b/solution.py
@@ -670,6 +670,38 @@
     sends += stage_x(lambda peer: mid_two.at[peer], answer, four_send, four_recv)
     answer[gx] = mid_two[gx]
     soil_step(6)
+
+    def store(source, target):
+        stores.append(pltpu.make_async_copy(source, target, out_sem.at[len(stores)]))
+        stores[-1].start()
+
+    for i in range(2):
+        store(
+            states[(STEPS + 1) % 2].at[i, pl.ds(PAD, cells)],
+            before_hbm.at[:, pl.ds(i * 128, 128)],
+        )
+    for side in range(2):
+
+        @pl.when(has[side])
+        def _():
+            for copy in cone_x(side):
+                copy.wait_send()
+
+        @pl.when(has[2 + side])
+        def _():
+            cone_y(side).wait_send()
+
+    for slot in range(STEPS):
+        for part in range(CHUNKS):
+            for side in range(4):
+
+                @pl.when(has[side])
+                def _():
+                    halo(slot, part, side).wait_send()
+
+    sent = len(sends) - (n_gx - 1)
+    for copy in sends[:sent]:
+        copy.wait_send()
     arrived_x(answer, four_send, four_recv)
 
     answer_t = jnp.concatenate(
@@ -698,42 +730,19 @@
         return unused
 
     lax.fori_loop(0, count // BLOCK, window, 0)
-    stores.append(pltpu.make_async_copy(disp_new, disp_out, out_sem.at[1]))
-    stores.append(pltpu.make_async_copy(vel_new, vel_out, out_sem.at[2]))
-    for copy in stores[1:]:
-        copy.start()
-
-    soil_step(7)
-    for state, output in ((states[STEPS % 2], next_hbm), (states[(STEPS + 1) % 2], before_hbm)):
+    store(disp_new, disp_out)
+    store(vel_new, vel_out)
+
+    for part in range(CHUNKS):
+        advance(STEPS - 1, part)
         for i in range(2):
-            stores.append(
-                pltpu.make_async_copy(
-                    state.at[i, pl.ds(PAD, cells)],
-                    output.at[:, pl.ds(i * 128, 128)],
-                    out_sem.at[len(stores)],
-                )
+            first, size = part * planes * rows, planes * rows
+            store(
+                states[STEPS % 2].at[i, pl.ds(PAD + first, size)],
+                next_hbm.at[pl.ds(first, size), pl.ds(i * 128, 128)],
             )
-            stores[-1].start()
-    for side in range(2):
-
-        @pl.when(has[side])
-        def _():
-            for copy in cone_x(side):
-                copy.wait_send()
-
-        @pl.when(has[2 + side])
-        def _():
-            cone_y(side).wait_send()
-
-    for copy in sends:
+    for copy in sends[sent:]:
         copy.wait_send()
-    for slot in range(STEPS):
-        for part in range(CHUNKS):
-            for side in range(4):
-
-                @pl.when(has[side])
-                def _():
-                    halo(slot, part, side).wait_send()
 
     for copy in stores:
         copy.wait()
@@ -743,7 +752,7 @@
     sources, targets, held, sems = refs[:5], refs[5:10], refs[10:15], refs[15:]
     ways = []
     for source, target, room in zip(sources, targets, held):
-        pieces = 2 if source.shape[0] > 256 else 1
+        pieces = 6 if source.shape[0] > 256 else 1
         size = source.shape[0] // pieces
         for i in range(pieces):
             part = pl.ds(i * size, size)
@@ -828,7 +837,7 @@
             vm((n_gx, n_gy, SLOTS * STEPS), f32),
             vm((n_gx, n_gy, SLOTS * STEPS), f32),
             dma((15,)),
-            dma((7,)),
+            dma((9,)),
             dma((STEPS, CHUNKS, 4)),
             dma((STEPS, CHUNKS, 4)),
             dma((4, 2)),
@@ -870,7 +879,7 @@
         out_shape=tuple(jax.ShapeDtypeStruct(a.shape, a.dtype) for a in out),
         in_specs=[hbm] * 5,
         out_specs=(hbm,) * 5,
-        scratch_shapes=[vm(a.shape, a.dtype) for a in out] + [dma((7,)), dma((7,))],
+        scratch_shapes=[vm(a.shape, a.dtype) for a in out] + [dma((15,)), dma((15,))],
         compiler_params=pltpu.CompilerParams(vmem_limit_bytes=62 * 1024 * 1024),
     )(*out)
     return (

time: 55.7 us -> 55.2 us (level)
  Pallas kernels: 54.9 us -> 54.3 us
    pallas_call x1, Pallas kernels: 51.8 us -> 51.1 us  [shards(): pl.pallas_call(functools.partial(kernel, n_gx, n_gy, depth, rows), out_sh...]
where the time goes in v5:
time: 55.2 us; the launch traced here: 55 us
  Pallas kernels  54.3 us (98%)
  between operations  0.64 us (1%)
    pallas_call x1, Pallas kernels, shards(): pl.pallas_call(functools.partial(kernel, n_gx, n_gy, depth, rows), out_sh...  51.1 us
    pallas_call x1, Pallas kernels, shards(): pl.pallas_call(hand_over, out_shape=tuple((jax.ShapeDtypeStruct(a.shape,...  3.28 us

profile of v5, /device:TPU:2, one launch (start us, length us, event | category | flops | bytes accessed | tf_op | source)
XLA Modules:
  0.0 55.0 jit_solution(14054120188763838487)
XLA Ops:
  0.6 51.1 %shard_map.137 = (f32[1536,256]{1,0:T(8,128)}, f32[1536,256]{1,0:T(8,128)}, f32[32,2048]{1,0:T(8,128)}, f32[32,2048]{1,0:T(8,128)}, f32[32,256]{1,0:T(8,128)}) custom-call(s32[1,2048]{1,0:T(1,128)} %bitcast.12, s32[1,2048]{1,0:T(1,128)} %bitcast.13, f32[1536,256]{1,0:T(8,128)} %bitcast.7, f32[1536,256]{1,0:T(8,128)} %bitcast.8, f32[1536,256]{1,0:T(8,128)} %bitcast.9, ...), custom_call_target="tpu_custom_call" | custom-call | flops 4000000000 | bytes 10000000 | tf_op jit(solution)/shard_map/pallas_call | solution.py:792
  51.7 3.3 %shard_map.138 = (f32[1536,256]{1,0:T(8,128)}, f32[1536,256]{1,0:T(8,128)}, f32[32,2048]{1,0:T(8,128)}, f32[32,2048]{1,0:T(8,128)}, f32[32,256]{1,0:T(8,128)}) custom-call(f32[1536,256]{1,0:T(8,128)} %get-tuple-element.15.refs_0_, f32[1536,256]{1,0:T(8,128)} %get-tuple-element.16.refs_1_, f32[32,2048]{1,0:T(8,128)} %get-tuple-element.17.refs_2_, ...), custom_call_target="tpu_custom_call" | custom-call | tf_op jit(solution)/shard_map/pallas_call | solution.py:877
